TPU v7x, 256 devices: a whole 4x4x8 slice. The times are simulated.
256 devices in a mesh: dp: 8 (over x, y_hi), ctx: 32 (over z, y_lo, core).
Axes of the slice: x: 4, y: 4 (y_hi: 2, y_lo: 2; y = y_hi * 2 + y_lo), z: 8, core: 2. Of those that a mesh axis runs over, the one named last changes fastest.
Arguments:
- qkv_pre: bfloat16 [3, 16, 2048, 4096], P(None, 'dp', 'ctx'), may hold values from -6 to 6
- d_out: bfloat16 [16, 2048, 4096], P('dp', 'ctx'), may hold values from -48 to 48
- inputs: bfloat16 [16, 2048, 4096], P('dp', 'ctx'), may hold values from -6 to 6
- conv_taps: float32 [3, 3, 4096], P(None, None, 'ctx'), may hold values from -0.2 to 1.4
- left_old: float32 [8, 32, 4, 128, 128], P('dp', 'ctx'), may hold values from -6 to 6
- right_old: float32 [8, 32, 4, 128, 128], P('dp', 'ctx'), may hold values from -6 to 6
Outputs:
- grad_qkv: bfloat16 [3, 16, 2048, 4096], P(None, 'dp', 'ctx')
- gram_left: float32 [8, 32, 4, 128, 128], P('dp', 'ctx')
- gram_right: float32 [8, 32, 4, 128, 128], P('dp', 'ctx')
All inputs are finite; a program needn't handle non-finite values.
Results may differ from a plain program's by a relative error of at most 0.012.
The roundings to bfloat16 on the way count: a program that leaves them out, or rounds other values in their place, can miss the bound.
Values may be sent and summed in bfloat16 or wider, within the bound.
No kernel may reach another device: no remote copies, remote signals or barrier semaphores. Data moves between devices by JAX's collectives and lax.ppermute only.
A program may use at most 128 MiB of HBM per device.

v0:
```python
import math

import jax
import jax.numpy as jnp
from jax import lax
from jax.sharding import PartitionSpec as P

HDIM = 128


BETA = 0.95


def from_behind(value, axis, by):
    count = lax.axis_size(axis)
    return lax.ppermute(value, axis, [(i, (i + by) % count) for i in range(count)])


def causal_conv(signal, tap_table):
    lag_one = jnp.pad(signal, ((0, 0), (1, 0), (0, 0)))[:, :-1]
    lag_two = jnp.pad(signal, ((0, 0), (2, 0), (0, 0)))[:, :-2]
    return tap_table[0] * signal + tap_table[1] * lag_one + tap_table[2] * lag_two


def conv_back(signal, tap_table):
    lead_one = jnp.pad(signal, ((0, 0), (0, 1), (0, 0)))[:, 1:]
    lead_two = jnp.pad(signal, ((0, 0), (0, 2), (0, 0)))[:, 2:]
    return tap_table[0] * signal + tap_table[1] * lead_one + tap_table[2] * lead_two


def head_blocks(query, key_rows, values, grad_rows):
    batch_size, length, head_width = query.shape
    scaling = 1.0 / math.sqrt(head_width)
    block_rows = 512
    d_keys = jnp.zeros((batch_size, length, head_width), jnp.float32)
    d_values = jnp.zeros((batch_size, length, head_width), jnp.float32)
    query_parts = []
    for block_index in range(length // block_rows):
        row_start = block_index * block_rows
        row_end = row_start + block_rows
        query_row_slab = query[:, row_start:row_end]
        visible_keys = key_rows[:, :row_end]
        visible_values = values[:, :row_end]
        output_row_slab = grad_rows[:, row_start:row_end]
        scores = (
            jnp.einsum(
                "yns,yhs->ynh", query_row_slab, visible_keys, preferred_element_type=jnp.float32
            )
            * scaling
        )
        row_ids = row_start + jnp.arange(block_rows)[:, None]
        col_ids = jnp.arange(row_end)[None, :]
        allowed = col_ids <= row_ids
        scores = jnp.where(allowed, scores, -jnp.inf)
        row_max = jnp.max(scores, axis=2, keepdims=True)
        exponent = jnp.where(allowed, jnp.exp(scores - row_max), 0.0)
        prob_full = exponent / jnp.sum(exponent, axis=2, keepdims=True)
        probability_halves = prob_full.astype(jnp.bfloat16)
        attention_weight_gradient = jnp.einsum(
            "yns,yhs->ynh", output_row_slab, visible_values, preferred_element_type=jnp.float32
        )
        row_inner = jnp.sum(prob_full * attention_weight_gradient, axis=2, keepdims=True)
        score_gradient = (prob_full * (attention_weight_gradient - row_inner)).astype(jnp.bfloat16)
        query_parts.append(
            jnp.einsum(
                "usm,umf->usf", score_gradient, visible_keys, preferred_element_type=jnp.float32
            )
            * scaling
        )
        d_keys = d_keys.at[:, :row_end].add(
            jnp.einsum(
                "pla,plm->pam", score_gradient, query_row_slab, preferred_element_type=jnp.float32
            )
            * scaling
        )
        d_values = d_values.at[:, :row_end].add(
            jnp.einsum(
                "pla,plm->pam",
                probability_halves,
                output_row_slab,
                preferred_element_type=jnp.float32,
            )
        )
    return (jnp.concatenate(query_parts, axis=1), d_keys, d_values)


def on_device(qkv_pre, d_out, inputs, conv_taps, left_old, right_old):
    triple, seq_count, tokens, channels = qkv_pre.shape
    ctx_size = lax.axis_size("ctx")
    dp_size = lax.axis_size("dp")
    span_size = ctx_size // dp_size
    flat_matrix = qkv_pre.reshape(triple * seq_count, tokens, channels)
    heads_in, grad_in, row_block = (
        lax.all_to_all(flat_matrix, "ctx", split_axis=2, concat_axis=1, tiled=True),
        lax.all_to_all(d_out, "ctx", split_axis=2, concat_axis=1, tiled=True),
        lax.all_to_all(inputs, "ctx", split_axis=2, concat_axis=1, tiled=True),
    )
    length = heads_in.shape[1]
    col_count = heads_in.shape[2]
    per_device = col_count // HDIM
    heads_in = heads_in.reshape(triple, seq_count, length, col_count)
    post_list = [
        causal_conv(heads_in[j].astype(jnp.float32), conv_taps[j]).astype(jnp.bfloat16)
        for j in range(3)
    ]

    def split_heads(matrix):
        return (
            matrix.reshape(seq_count, length, per_device, HDIM)
            .transpose(0, 2, 1, 3)
            .reshape(seq_count * per_device, length, HDIM)
        )

    def join_heads(stacked):
        return (
            stacked.reshape(seq_count, per_device, length, HDIM)
            .transpose(0, 2, 1, 3)
            .reshape(seq_count, length, col_count)
        )

    d_query, d_keys, d_values = head_blocks(
        split_heads(post_list[0]),
        split_heads(post_list[1]),
        split_heads(post_list[2]),
        split_heads(grad_in),
    )
    grad_heads = jnp.stack(
        [
            conv_back(join_heads(gradient), conv_taps[j]).astype(jnp.bfloat16)
            for j, gradient in enumerate((d_query, d_keys, d_values))
        ]
    )
    returned = lax.all_to_all(
        grad_heads.reshape(triple * seq_count, length, col_count),
        "ctx",
        split_axis=1,
        concat_axis=2,
        tiled=True,
    )
    grad_qkv = returned.reshape(triple, seq_count, tokens, channels)
    row_list = [row_block]
    for offset in range(1, span_size):
        row_list.append(from_behind(row_block, "ctx", offset))
    row_stack = jnp.stack(row_list)
    query_grad = grad_heads[0]
    col_list = [query_grad]
    for hop_index in range(1, dp_size):
        col_list.append(from_behind(query_grad, "ctx", span_size * hop_index))
    col_stack = jnp.stack(col_list)
    summed = lax.psum_scatter(
        jnp.einsum(
            "kabc,sabr->ksrc", col_stack, row_stack, preferred_element_type=jnp.float32
        ).astype(jnp.bfloat16),
        "dp",
        scatter_dimension=0,
        tiled=True,
    ).astype(jnp.float32)
    token_total = seq_count * dp_size * length
    grad_tiles = summed[0] * (1.0 / math.sqrt(token_total))
    left_new = BETA * left_old[0, 0] + (1.0 - BETA) * jnp.einsum(
        "srk,sqk->srq", grad_tiles, grad_tiles, precision=lax.Precision.HIGHEST
    )
    right_new = BETA * right_old[0, 0] + (1.0 - BETA) * jnp.einsum(
        "srk,srq->skq", grad_tiles, grad_tiles, precision=lax.Precision.HIGHEST
    )
    return (grad_qkv, left_new[None, None], right_new[None, None])


def solution(mesh):
    return jax.shard_map(
        on_device,
        mesh=mesh,
        in_specs=(
            P(None, "dp", "ctx", None),
            P("dp", "ctx", None),
            P("dp", "ctx", None),
            P(None, None, "ctx"),
            P("dp", "ctx", None, None, None),
            P("dp", "ctx", None, None, None),
        ),
        out_specs=(
            P(None, "dp", "ctx", None),
            P("dp", "ctx", None, None, None),
            P("dp", "ctx", None, None, None),
        ),
        check_vma=False,
    )
```

profile of v0, /device:TPU:46, one launch (start us, length us, event | category | flops | bytes accessed | tf_op | source)
XLA Modules:
  0.0 683.2 jit_solution(14081230235818318958)
XLA Ops:
  14.5 9.6 %all-to-all-start.1 = ((bf16[32,2,8192]{2,1,0:T(2,128)(2,1)}), bf16[32,2,8192]{2,1,0:T(2,128)(2,1)S(1)}, u32[]{:S(2)}, u32[]{:S(2)}) async-start(bf16[32,2,8192]{2,1,0:T(2,128)(2,1)} %reshape.330), calls=%async_computation.1 | async-start | bytes 2097152 | tf_op jit(solution)/shard_map/all_to_all | solution.py:95
  31.4 20.8 %all-to-all-done.1 = bf16[32,2,8192]{2,1,0:T(2,128)(2,1)S(1)} async-done(((bf16[32,2,8192]{2,1,0:T(2,128)(2,1)}), bf16[32,2,8192]{2,1,0:T(2,128)(2,1)S(1)}, u32[]{:S(2)}, u32[]{:S(2)}) %all-to-all-start.1) | async-done | bytes 1048608 | tf_op jit(solution)/shard_map/all_to_all | solution.py:95
  57.1 9.8 %copy.93 = bf16[6,64,4096]{1,0,2:T(8,128)(2,1)} copy(bf16[6,64,4096]{2,1,0:T(8,128)(2,1)} %bitcast.180) | data formatting | bytes 6291456 | tf_op jit(solution)/shard_map/reshape | solution.py:92
  66.9 12.9 %reshape.332 = bf16[32,2,24576]{2,1,0:T(2,128)(2,1)} reshape(bf16[4096,6,64]{2,1,0:T(8,128)(2,1)} %bitcast.163) | data formatting | bytes 6291456
  79.8 5.4 all-to-all-done.3
  95.8 5.7 reshape.335
  101.5 5.4 copy.136
  111.3 5.7 reshape.331
  117.0 5.4 copy.99
  124.7 39.7 %all-to-all-done = bf16[32,2,24576]{2,1,0:T(2,128)(2,1)S(1)} async-done(((bf16[32,2,24576]{2,1,0:T(2,128)(2,1)}), bf16[32,2,24576]{2,1,0:T(2,128)(2,1)S(1)}, u32[]{:S(2)}, u32[]{:S(2)}) %all-to-all-start) | async-done | bytes 3145760 | tf_op jit(solution)/shard_map/all_to_all | solution.py:94
  164.5 7.1 %reshape.333 = bf16[4096,6,64]{2,1,0:T(8,128)(2,1)} reshape(bf16[32,2,24576]{2,1,0:T(2,128)(2,1)S(1)} %all-to-all-done) | data formatting | bytes 6291456
  171.5 7.3 %copy.134 = bf16[6,64,32,128]{3,2,1,0:T(8,128)(2,1)S(1)} copy(bf16[6,64,32,128]{1,0,3,2:T(8,128)(2,1)} %bitcast.162) | data formatting | bytes 6291456 | tf_op jit(solution)/shard_map/all_to_all | solution.py:94
  189.9 5.7 fusion.195
  195.6 8.9 %fusion.200 = (f32[2,512]{1,0:T(2,128)S(1)}, f32[2,512,2048]{2,1,0:T(8,128)}) fusion(pred[512,2048]{1,0:T(8,128)(4,1)} %iota_compare_fusion, bf16[2,2048,128]{2,1,0:T(8,128)(2,1)S(1)} %get-tuple-element.148, bf16[2,2048,128]{2,1,0:T(8,128)(2,1)} %copy-done.1), kind=kOutput, calls=%fused_computation.229 | convolution fusion | flops 547358720 | bytes 11800576 | tf_op jit(solution)/shard_map/sub | solution.py:56
  266.2 13.4 %copy.110 = bf16[6,2048,128]{2,0,1:T(8,128)(2,1)} copy(bf16[6,2048,128]{2,1,0:T(8,128)(2,1)S(1)} %bitcast.164) | data formatting | bytes 6291456 | tf_op jit(solution)/shard_map/reshape | solution.py:134
  279.6 8.4 %all-to-all-start.2 = ((bf16[6,2048,128]{2,0,1:T(8,128)(2,1)}), bf16[6,2048,128]{2,0,1:T(8,128)(2,1)}, u32[]{:S(2)}, u32[]{:S(2)}) async-start(bf16[6,2048,128]{2,0,1:T(8,128)(2,1)} %copy.110), calls=%async_computation.2 | async-start | bytes 8388608 | tf_op jit(solution)/shard_map/all_to_all | solution.py:133
  294.9 42.8 %collective-permute-done.4 = bf16[2,2048,128]{2,1,0:T(8,128)(2,1)S(1)} collective-permute-done((bf16[2,2048,128]{2,1,0:T(8,128)(2,1)S(1)}, bf16[2,2048,128]{2,1,0:T(8,128)(2,1)S(1)}, u32[]{:S(2)}, u32[]{:S(2)}) %collective-permute-start.4) | collective-permute-done | bytes 1048608 | tf_op jit(solution)/shard_map/ppermute | solution.py:16
  338.8 54.5 %collective-permute-done.5 = bf16[2,2048,128]{2,1,0:T(8,128)(2,1)S(1)} collective-permute-done((bf16[2,2048,128]{2,1,0:T(8,128)(2,1)S(1)}, bf16[2,2048,128]{2,1,0:T(8,128)(2,1)S(1)}, u32[]{:S(2)}, u32[]{:S(2)}) %collective-permute-start.5) | collective-permute-done | bytes 1048608 | tf_op jit(solution)/shard_map/ppermute | solution.py:16
  393.3 10.2 %collective-permute-start.8 = (bf16[2,2048,128]{2,1,0:T(8,128)(2,1)S(1)}, bf16[2,2048,128]{2,1,0:T(8,128)(2,1)S(1)}, u32[]{:S(2)}, u32[]{:S(2)}) collective-permute-start(bf16[2,2048,128]{2,1,0:T(8,128)(2,1)S(1)} %get-tuple-element.116), channel_id=1, source_target_pairs={{0,24},{1,25},{2,26},{3,27},{4,28},{5,29},{6,30},{7,31},{8,0},{9,1... | collective-permute-start | bytes 3145736 | tf_op jit(solution)/shard_map/ppermute | solution.py:16
  404.5 24.8 %collective-permute-done.6 = bf16[2,2048,128]{2,1,0:T(8,128)(2,1)S(1)} collective-permute-done((bf16[2,2048,128]{2,1,0:T(8,128)(2,1)S(1)}, bf16[2,2048,128]{2,1,0:T(8,128)(2,1)S(1)}, u32[]{:S(2)}, u32[]{:S(2)}) %collective-permute-start.6) | collective-permute-done | bytes 1048608 | tf_op jit(solution)/shard_map/ppermute | solution.py:16
  429.3 100.0 %collective-permute-start.9 = (bf16[2,2048,128]{2,1,0:T(8,128)(2,1)S(1)}, bf16[2,2048,128]{2,1,0:T(8,128)(2,1)S(1)}, u32[]{:S(2)}, u32[]{:S(2)}) collective-permute-start(bf16[2,2048,128]{2,1,0:T(8,128)(2,1)S(1)} %get-tuple-element.116), channel_id=1, source_target_pairs={{0,28},{1,29},{2,30},{3,31},{4,0},{5,1},{6,2},{7,3},{8,4},{9,5},{1... | collective-permute-start | bytes 3145736 | tf_op jit(solution)/shard_map/ppermute | solution.py:16
  532.8 27.4 %collective-permute-done.9 = bf16[2,2048,128]{2,1,0:T(8,128)(2,1)S(1)} collective-permute-done((bf16[2,2048,128]{2,1,0:T(8,128)(2,1)S(1)}, bf16[2,2048,128]{2,1,0:T(8,128)(2,1)S(1)}, u32[]{:S(2)}, u32[]{:S(2)}) %collective-permute-start.9) | collective-permute-done | bytes 1048608 | tf_op jit(solution)/shard_map/ppermute | solution.py:16
  561.4 9.6 %fusion.87 = bf16[8,4,128,128]{3,2,0,1:T(8,128)(2,1)} fusion(bf16[8,2,2048,128]{3,2,1,0:T(8,128)(2,1)} %bitcast_dynamic-update-slice_fusion, bf16[1,2,2048,128]{2,3,1,0:T(8,128)(2,1)S(1)} %bitcast.189, bf16[1,2,2048,128]{2,3,1,0:T(8,128)(2,1)} %bitcast.38, bf16[1,2,2048,128]{2,3,1,0:T(8,128)(2,1)} %bitcast.36, bf16[1,2,2048,128]{2,3,1,0:T(8,128)(2,1)S(1)} %copy-done.13), kind=kOutput, calls=%fused_computation.119 | convolution fusion | flops 4312268800 | bytes 13631488 | tf_op jit(solution)/shard_map/kabc,sabr->ksrc/dot_general | solution.py:151
  571.7 91.0 %all-reduce.17.cloned.1.call-done = bf16[8,4,128,128]{3,2,0,1:T(8,128)(2,1)} async-done(((bf16[8,4,128,128]{3,2,0,1:T(8,128)(2,1)}), bf16[8,4,128,128]{3,2,0,1:T(8,128)(2,1)}) %all-reduce.17.cloned.1.call-update) | async-done | bytes 1048592
  (132 shorter events, 137.0 us)
Async XLA Ops:
  14.5 37.7 %all-to-all-start.1 = ((bf16[32,2,8192]{2,1,0:T(2,128)(2,1)}), bf16[32,2,8192]{2,1,0:T(2,128)(2,1)S(1)}, u32[]{:S(2)}, u32[]{:S(2)}) async-start(bf16[32,2,8192]{2,1,0:T(2,128)(2,1)} %reshape.330), calls=%async_computation.1 | async-start | bytes 2097152 | tf_op jit(solution)/shard_map/all_to_all | solution.py:95
  52.2 14.7 %copy-start.3 = (bf16[32,2,8192]{2,1,0:T(2,128)(2,1)}, bf16[32,2,8192]{2,1,0:T(2,128)(2,1)S(1)}, u32[]{:S(2)}) copy-start(bf16[32,2,8192]{2,1,0:T(2,128)(2,1)S(1)} %all-to-all-done.1) | copy-start | bytes 3145732
  52.2 33.0 %all-to-all-start.3 = ((bf16[32,2,8192]{2,1,0:T(2,128)(2,1)}), bf16[32,2,8192]{2,1,0:T(2,128)(2,1)S(1)}, u32[]{:S(2)}, u32[]{:S(2)}) async-start(bf16[32,2,8192]{2,1,0:T(2,128)(2,1)} %reshape.334), calls=%async_computation.3 | async-start | bytes 2097152 | tf_op jit(solution)/shard_map/all_to_all | solution.py:96
  79.8 11.7 %copy-start.19 = (f32[3,3,128]{2,1,0:T(4,128)S(1)}, f32[3,3,128]{2,1,0:T(4,128)}, u32[]{:S(2)}) copy-start(f32[3,3,128]{2,1,0:T(4,128)} %param.29) | copy-start | bytes 13828
  86.2 78.2 %all-to-all-start = ((bf16[32,2,24576]{2,1,0:T(2,128)(2,1)}), bf16[32,2,24576]{2,1,0:T(2,128)(2,1)S(1)}, u32[]{:S(2)}, u32[]{:S(2)}) async-start(bf16[32,2,24576]{2,1,0:T(2,128)(2,1)} %reshape.332), calls=%async_computation | async-start | bytes 6291456 | tf_op jit(solution)/shard_map/all_to_all | solution.py:94
  109.2 452.1 %collective-permute-start = (bf16[2,2048,128]{1,2,0:T(8,128)(2,1)}, bf16[2,2048,128]{1,2,0:T(8,128)(2,1)}, u32[]{:S(2)}, u32[]{:S(2)}) collective-permute-start(bf16[2,2048,128]{1,2,0:T(8,128)(2,1)} %copy.116), channel_id=1, source_target_pairs={{0,1},{1,2},{2,3},{3,4},{4,5},{5,6},{6,7},{7,8},{8,9},{9,10},{10,1... | collective-permute-start | bytes 3145736 | tf_op jit(solution)/shard_map/ppermute | solution.py:16
  109.4 452.0 %collective-permute-start.1 = (bf16[2,2048,128]{1,2,0:T(8,128)(2,1)}, bf16[2,2048,128]{1,2,0:T(8,128)(2,1)}, u32[]{:S(2)}, u32[]{:S(2)}) collective-permute-start(bf16[2,2048,128]{1,2,0:T(8,128)(2,1)} %copy.116), channel_id=1, source_target_pairs={{0,2},{1,3},{2,4},{3,5},{4,6},{5,7},{6,8},{7,9},{8,10},{9,11},{10,... | collective-permute-start | bytes 3145736 | tf_op jit(solution)/shard_map/ppermute | solution.py:16
  195.6 8.9 %copy-start = (f32[2,32,64,128]{3,1,2,0:T(8,128)S(1)}, f32[2,32,64,128]{3,1,2,0:T(8,128)}, u32[]{:S(2)}) copy-start(f32[2,32,64,128]{3,1,2,0:T(8,128)} %get-tuple-element.117) | copy-start | bytes 6291460
  211.8 18.9 %copy-start.6 = (f32[2,512,1024]{2,1,0:T(8,128)}, f32[2,512,1024]{2,1,0:T(8,128)S(1)}, u32[]{:S(2)}) copy-start(f32[2,512,1024]{2,1,0:T(8,128)S(1)} %get-tuple-element.134) | copy-start | bytes 12582916
  256.1 32.0 %collective-permute-start.3 = (bf16[2,2048,128]{2,1,0:T(8,128)(2,1)S(1)}, bf16[2,2048,128]{2,1,0:T(8,128)(2,1)}, u32[]{:S(2)}, u32[]{:S(2)}) collective-permute-start(bf16[2,2048,128]{2,1,0:T(8,128)(2,1)S(1)} %get-tuple-element.116), channel_id=1, source_target_pairs={{0,4},{1,5},{2,6},{3,7},{4,8},{5,9},{6,10},{7,11},{8,12},{9,13},{1... | collective-permute-start | bytes 3145736 | tf_op jit(solution)/shard_map/ppermute | solution.py:16
  257.2 80.6 %collective-permute-start.4 = (bf16[2,2048,128]{2,1,0:T(8,128)(2,1)S(1)}, bf16[2,2048,128]{2,1,0:T(8,128)(2,1)S(1)}, u32[]{:S(2)}, u32[]{:S(2)}) collective-permute-start(bf16[2,2048,128]{2,1,0:T(8,128)(2,1)S(1)} %get-tuple-element.116), channel_id=1, source_target_pairs={{0,8},{1,9},{2,10},{3,11},{4,12},{5,13},{6,14},{7,15},{8,16},{9,17... | collective-permute-start | bytes 3145736 | tf_op jit(solution)/shard_map/ppermute | solution.py:16
  257.2 136.1 %collective-permute-start.5 = (bf16[2,2048,128]{2,1,0:T(8,128)(2,1)S(1)}, bf16[2,2048,128]{2,1,0:T(8,128)(2,1)S(1)}, u32[]{:S(2)}, u32[]{:S(2)}) collective-permute-start(bf16[2,2048,128]{2,1,0:T(8,128)(2,1)S(1)} %get-tuple-element.116), channel_id=1, source_target_pairs={{0,12},{1,13},{2,14},{3,15},{4,16},{5,17},{6,18},{7,19},{8,20},{9,... | collective-permute-start | bytes 3145736 | tf_op jit(solution)/shard_map/ppermute | solution.py:16
  279.6 389.0 %all-to-all-start.2 = ((bf16[6,2048,128]{2,0,1:T(8,128)(2,1)}), bf16[6,2048,128]{2,0,1:T(8,128)(2,1)}, u32[]{:S(2)}, u32[]{:S(2)}) async-start(bf16[6,2048,128]{2,0,1:T(8,128)(2,1)} %copy.110), calls=%async_computation.2 | async-start | bytes 8388608 | tf_op jit(solution)/shard_map/all_to_all | solution.py:133
  288.0 374.6 %all-reduce.17.cloned.1.call-start = ((), (), s32[]{:S(2)}) async-start(), calls=%async_computation.4 | async-start | bytes 2097152
  288.1 141.2 %collective-permute-start.6 = (bf16[2,2048,128]{2,1,0:T(8,128)(2,1)S(1)}, bf16[2,2048,128]{2,1,0:T(8,128)(2,1)S(1)}, u32[]{:S(2)}, u32[]{:S(2)}) collective-permute-start(bf16[2,2048,128]{2,1,0:T(8,128)(2,1)S(1)} %get-tuple-element.116), channel_id=1, source_target_pairs={{0,16},{1,17},{2,18},{3,19},{4,20},{5,21},{6,22},{7,23},{8,24},{9,... | collective-permute-start | bytes 3145736 | tf_op jit(solution)/shard_map/ppermute | solution.py:16
  294.9 235.5 %copy-start.12 = (bf16[2,2048,128]{1,2,0:T(8,128)(2,1)S(1)}, bf16[2,2048,128]{1,2,0:T(8,128)(2,1)}, u32[]{:S(2)}) copy-start(bf16[2,2048,128]{1,2,0:T(8,128)(2,1)} %copy.116) | copy-start | bytes 3145732
  337.7 192.7 %collective-permute-start.7 = (bf16[2,2048,128]{2,1,0:T(8,128)(2,1)S(1)}, bf16[2,2048,128]{2,1,0:T(8,128)(2,1)S(1)}, u32[]{:S(2)}, u32[]{:S(2)}) collective-permute-start(bf16[2,2048,128]{2,1,0:T(8,128)(2,1)S(1)} %get-tuple-element.116), channel_id=1, source_target_pairs={{0,20},{1,21},{2,22},{3,23},{4,24},{5,25},{6,26},{7,27},{8,28},{9,... | collective-permute-start | bytes 3145736 | tf_op jit(solution)/shard_map/ppermute | solution.py:16
  393.3 138.5 %collective-permute-start.8 = (bf16[2,2048,128]{2,1,0:T(8,128)(2,1)S(1)}, bf16[2,2048,128]{2,1,0:T(8,128)(2,1)S(1)}, u32[]{:S(2)}, u32[]{:S(2)}) collective-permute-start(bf16[2,2048,128]{2,1,0:T(8,128)(2,1)S(1)} %get-tuple-element.116), channel_id=1, source_target_pairs={{0,24},{1,25},{2,26},{3,27},{4,28},{5,29},{6,30},{7,31},{8,0},{9,1... | collective-permute-start | bytes 3145736 | tf_op jit(solution)/shard_map/ppermute | solution.py:16
  429.3 130.9 %collective-permute-start.9 = (bf16[2,2048,128]{2,1,0:T(8,128)(2,1)S(1)}, bf16[2,2048,128]{2,1,0:T(8,128)(2,1)S(1)}, u32[]{:S(2)}, u32[]{:S(2)}) collective-permute-start(bf16[2,2048,128]{2,1,0:T(8,128)(2,1)S(1)} %get-tuple-element.116), channel_id=1, source_target_pairs={{0,28},{1,29},{2,30},{3,31},{4,0},{5,1},{6,2},{7,3},{8,4},{9,5},{1... | collective-permute-start | bytes 3145736 | tf_op jit(solution)/shard_map/ppermute | solution.py:16
  530.4 30.9 %copy-start.13 = (bf16[1,2,2048,128]{2,3,1,0:T(8,128)(2,1)S(1)}, bf16[1,2,2048,128]{2,3,1,0:T(8,128)(2,1)}, u32[]{:S(2)}) copy-start(bf16[1,2,2048,128]{2,3,1,0:T(8,128)(2,1)} %copy.119) | copy-start | bytes 3145732
  530.4 30.9 %collective-permute-start.2 = (bf16[2,2048,128]{1,2,0:T(8,128)(2,1)S(1)}, bf16[2,2048,128]{1,2,0:T(8,128)(2,1)S(1)}, u32[]{:S(2)}, u32[]{:S(2)}) collective-permute-start(bf16[2,2048,128]{1,2,0:T(8,128)(2,1)S(1)} %copy-done.12), channel_id=1, source_target_pairs={{0,3},{1,4},{2,5},{3,6},{4,7},{5,8},{6,9},{7,10},{8,11},{9,12},{10... | collective-permute-start | bytes 3145736 | tf_op jit(solution)/shard_map/ppermute | solution.py:16
  561.4 9.6 %copy-start.20 = (u32[256]{0:T(256)S(1)}, u32[256]{0:T(256)}, u32[]{:S(2)}) copy-start(u32[256]{0:T(256)} %constant.260) | copy-start | bytes 3076
  561.4 101.3 %copy-start.17 = (f32[1,1,4,128,128]{4,3,2,1,0:T(8,128)S(1)}, f32[1,1,4,128,128]{4,3,2,1,0:T(8,128)}, u32[]{:S(2)}) copy-start(f32[1,1,4,128,128]{4,3,2,1,0:T(8,128)} %param.30) | copy-start | bytes 786436
  561.4 104.3 %copy-start.18 = (f32[1,1,4,128,128]{4,3,2,1,0:T(8,128)S(1)}, f32[1,1,4,128,128]{4,3,2,1,0:T(8,128)}, u32[]{:S(2)}) copy-start(f32[1,1,4,128,128]{4,3,2,1,0:T(8,128)} %param.31) | copy-start | bytes 786436
  (16 other events, 56.2 us)
Sparse Core Ops, SparseCore 0:
  571.1 91.5 all-reduce.16
where the time goes:
time: 695 us; the launch traced here: 683 us
  waiting for transfers between devices  306 us (44%)
  starting transfers between devices  148 us (21%)
  local copies, waits for them, and re-layouts  118 us (17%)
  matrix products  66.7 us (10%)
  other arithmetic  28.6 us (4%)
  between operations  14.7 us (2%)
    ppermute x10, waiting for transfers between devices, from_behind(): lax.ppermute(value, axis, [(i, (i + by) % count) for i in range(count)])  149 us
    ppermute x10, starting transfers between devices, from_behind(): lax.ppermute(value, axis, [(i, (i + by) % count) for i in range(count)])  120 us
    unnamed x2, waiting for transfers between devices  91 us
    unnamed x65, local copies, waits for them, and re-layouts  58.5 us
    all_to_all x1, waiting for transfers between devices, on_device(): lax.all_to_all(flat_matrix, 'ctx', split_axis=2, concat_axis=1, tiled=True)  39.7 us
    all_to_all x1, waiting for transfers between devices, on_device(): lax.all_to_all(d_out, 'ctx', split_axis=2, concat_axis=1, tiled=True)  20.8 us
    sub x3, matrix products, head_blocks(): exponent = jnp.where(allowed, jnp.exp(scores - row_max), 0.0)  17 us
  transfers between devices with their start and end apart: 15, of which 8 were waited for; matrix products, arithmetic and copies ran while one was open for 28% of the time, Pallas kernels for 0%

commit v1 on v0

v1 whole, which is shorter than its diff:
```python
import math

import jax
import jax.numpy as jnp
from jax import lax
from jax.experimental import pallas as pl
from jax.experimental.pallas import tpu as pltpu
from jax.sharding import Mesh, PartitionSpec as P

HDIM = 128
BETA = 0.95

DP = ("x", "yh")
CTX = ("z", "yl", "core")
PLANE = ("x", "yh", "yl", "core")
ALL = ("x", "yh", "z", "yl", "core")
N_Z = 8
N_CTX = 32
N_DP = 8
SPAN = 4
TOK = 64
LEN = N_CTX * TOK
BLOCK = 256
PAD = 8


def nt_dot(a, b):
    return lax.dot_general(a, b, (((1,), (1,)), ((), ())), preferred_element_type=jnp.float32)


def nn_dot(a, b):
    return lax.dot_general(a, b, (((1,), (0,)), ((), ())), preferred_element_type=jnp.float32)


def pack_kernel(qkv_ref, dout_ref, out_ref):
    width = out_ref.shape[0]
    for c in range(width):
        lanes = slice(c * HDIM, (c + 1) * HDIM)
        for j in range(3):
            out_ref[c, j * TOK : (j + 1) * TOK, :] = qkv_ref[j, 0, :, lanes]
        out_ref[c, 3 * TOK : 4 * TOK, :] = dout_ref[0, :, lanes]


def pack(qkv_pre, d_out, seq, width=8):
    return pl.pallas_call(
        pack_kernel,
        grid=(N_CTX // width,),
        in_specs=[
            pl.BlockSpec((3, 1, TOK, width * HDIM), lambda i: (0, seq, 0, i)),
            pl.BlockSpec((1, TOK, width * HDIM), lambda i: (seq, 0, i)),
        ],
        out_specs=pl.BlockSpec((width, 4 * TOK, HDIM), lambda i: (i, 0, 0)),
        out_shape=jax.ShapeDtypeStruct((N_CTX, 4 * TOK, HDIM), jnp.bfloat16),
        name=f"pack{seq}",
        cost_estimate=pl.CostEstimate(flops=0, bytes_accessed=4 << 20, transcendentals=0),
    )(qkv_pre, d_out)


def attention_kernel(
    recv_ref, taps_ref, gq_ref, gkv_ref, pad_ref, post_ref, kt_ref, s_ref, w_ref, grad_ref
):
    scale = 1.0 / math.sqrt(HDIM)
    factor = scale * math.log2(math.e)
    pad_ref[0:PAD, :] = jnp.zeros((PAD, HDIM), jnp.float32)
    for j in range(3):
        signal = recv_ref[:, j * TOK : (j + 1) * TOK, :].reshape(LEN, HDIM).astype(jnp.float32)
        pad_ref[PAD : PAD + LEN, :] = signal
        mixed = (
            taps_ref[j, 0:1, :] * signal
            + taps_ref[j, 1:2, :] * pad_ref[PAD - 1 : PAD - 1 + LEN, :]
            + taps_ref[j, 2:3, :] * pad_ref[PAD - 2 : PAD - 2 + LEN, :]
        )
        post_ref[j] = mixed.astype(jnp.bfloat16)
        if j == 1:
            kt_ref[...] = jnp.transpose(post_ref[1].astype(jnp.float32)).astype(jnp.bfloat16)
    grad_ref[...] = jnp.zeros_like(grad_ref)

    key_ids = lax.broadcasted_iota(jnp.int32, (BLOCK, BLOCK), 0)
    query_ids = lax.broadcasted_iota(jnp.int32, (BLOCK, BLOCK), 1)
    per_block = BLOCK // TOK
    for i in range(LEN // BLOCK):
        rows = slice(i * BLOCK, (i + 1) * BLOCK)
        query = post_ref[0, rows, :]
        d_out = recv_ref[i * per_block : (i + 1) * per_block, 3 * TOK : 4 * TOK, :].reshape(
            BLOCK, HDIM
        )
        top = None
        for j in range(i + 1):
            cols = slice(j * BLOCK, (j + 1) * BLOCK)
            scores = nt_dot(post_ref[1, cols, :], query)
            if j == i:
                scores = jnp.where(key_ids <= query_ids, scores, -jnp.inf)
            s_ref[cols, :] = scores
            part = jnp.max(scores, axis=0, keepdims=True)
            top = part if top is None else jnp.maximum(top, part)
        total = jnp.zeros((1, BLOCK), jnp.float32)
        inner = jnp.zeros((1, BLOCK), jnp.float32)
        for j in range(i + 1):
            cols = slice(j * BLOCK, (j + 1) * BLOCK)
            exponent = jnp.exp2((s_ref[cols, :] - top) * factor)
            weights = nt_dot(post_ref[2, cols, :], d_out)
            s_ref[cols, :] = exponent
            w_ref[cols, :] = weights
            total = total + jnp.sum(exponent, axis=0, keepdims=True)
            inner = inner + jnp.sum(exponent * weights, axis=0, keepdims=True)
        inverse = 1.0 / total
        inner = inner * inverse
        dq_t = jnp.zeros((HDIM, BLOCK), jnp.float32)
        for j in range(i + 1):
            cols = slice(j * BLOCK, (j + 1) * BLOCK)
            prob = s_ref[cols, :] * inverse
            d_scores = (prob * (w_ref[cols, :] - inner)).astype(jnp.bfloat16)
            grad_ref[1, cols, :] += nn_dot(d_scores, query)
            grad_ref[2, cols, :] += nn_dot(prob.astype(jnp.bfloat16), d_out)
            dq_t = dq_t + nn_dot(kt_ref[:, cols], d_scores)
        grad_ref[0, rows, :] = jnp.transpose(dq_t)

    for j in range(3):
        factor_back = scale if j < 2 else 1.0
        grads = (
            taps_ref[j, 0:1, :] * (grad_ref[j, 0:LEN, :] * factor_back)
            + taps_ref[j, 1:2, :] * (grad_ref[j, 1 : LEN + 1, :] * factor_back)
            + taps_ref[j, 2:3, :] * (grad_ref[j, 2 : LEN + 2, :] * factor_back)
        )
        halves = grads.astype(jnp.bfloat16).reshape(N_CTX, TOK, HDIM)
        if j == 0:
            gq_ref[...] = halves
        else:
            gkv_ref[:, (j - 1) * TOK : j * TOK, :] = halves


def attention(received, taps, seq):
    vmem = pl.BlockSpec(memory_space=pltpu.VMEM)
    return pl.pallas_call(
        attention_kernel,
        in_specs=[vmem, vmem],
        out_specs=[vmem, vmem],
        out_shape=[
            jax.ShapeDtypeStruct((N_CTX, TOK, HDIM), jnp.bfloat16),
            jax.ShapeDtypeStruct((N_CTX, 2 * TOK, HDIM), jnp.bfloat16),
        ],
        scratch_shapes=[
            pltpu.VMEM((LEN + PAD, HDIM), jnp.float32),
            pltpu.VMEM((3, LEN, HDIM), jnp.bfloat16),
            pltpu.VMEM((HDIM, LEN), jnp.bfloat16),
            pltpu.VMEM((LEN, BLOCK), jnp.float32),
            pltpu.VMEM((LEN, BLOCK), jnp.float32),
            pltpu.VMEM((3, LEN + PAD, HDIM), jnp.float32),
        ],
        compiler_params=pltpu.CompilerParams(vmem_limit_bytes=32 << 20),
        name=f"attention{seq}",
        cost_estimate=pl.CostEstimate(
            flops=6 * LEN * LEN * HDIM, bytes_accessed=4 << 20, transcendentals=LEN * LEN // 2
        ),
    )(received, taps)


def unpack_kernel(q0_ref, kv0_ref, q1_ref, kv1_ref, out_ref):
    for c in range(q0_ref.shape[0]):
        lanes = slice(c * HDIM, (c + 1) * HDIM)
        for seq, (q_ref, kv_ref) in enumerate(((q0_ref, kv0_ref), (q1_ref, kv1_ref))):
            out_ref[0, seq, :, lanes] = q_ref[c]
            out_ref[1, seq, :, lanes] = kv_ref[c, 0:TOK, :]
            out_ref[2, seq, :, lanes] = kv_ref[c, TOK : 2 * TOK, :]


def unpack(q0, kv0, q1, kv1, width=8):
    q_spec = pl.BlockSpec((width, TOK, HDIM), lambda i: (i, 0, 0))
    kv_spec = pl.BlockSpec((width, 2 * TOK, HDIM), lambda i: (i, 0, 0))
    return pl.pallas_call(
        unpack_kernel,
        grid=(N_CTX // width,),
        in_specs=[q_spec, kv_spec, q_spec, kv_spec],
        out_specs=pl.BlockSpec((3, 2, TOK, width * HDIM), lambda i: (0, 0, 0, i)),
        out_shape=jax.ShapeDtypeStruct((3, 2, TOK, N_CTX * HDIM), jnp.bfloat16),
        name="unpack",
        cost_estimate=pl.CostEstimate(flops=0, bytes_accessed=6 << 20, transcendentals=0),
    )(q0, kv0, q1, kv1)


FEATS = 512


def tiles_first_kernel(grad_ref, x_ref, out_ref, gt_ref):
    @pl.when(pl.program_id(0) == 0)
    def _():
        full = grad_ref[...].reshape(LEN, HDIM).astype(jnp.float32)
        gt_ref[...] = jnp.transpose(full).astype(jnp.bfloat16)

    out_ref[...] = nn_dot(gt_ref[...], x_ref[:, 0].reshape(LEN, FEATS))


def tiles_second_kernel(lane_ref, grad_ref, x_ref, first_ref, out_ref, gt_ref):
    step = pl.program_id(0)

    @pl.when(step == 0)
    def _():
        full = grad_ref[...].reshape(LEN, HDIM).astype(jnp.float32)
        gt_ref[...] = jnp.transpose(full).astype(jnp.bfloat16)

    done = (first_ref[...] + nn_dot(gt_ref[...], x_ref[:, 0].reshape(LEN, FEATS))).astype(
        jnp.bfloat16
    )
    for k in range(FEATS // HDIM):
        ahead = (step * (FEATS // HDIM) + k - lane_ref[0] + N_CTX) & (N_CTX - 1)
        offset = (SPAN - (ahead & (SPAN - 1))) & (SPAN - 1)
        plane = ((ahead + SPAN - 1) // SPAN) & (N_Z - 1)
        out_ref[plane * SPAN + offset] = done[:, k * HDIM : (k + 1) * HDIM]


def tile_sums(grad0, grad1, gathered, lane):
    steps = N_CTX * HDIM // FEATS
    cost = pl.CostEstimate(
        flops=2 * LEN * HDIM * HDIM * N_CTX, bytes_accessed=20 << 20, transcendentals=0
    )
    grad_spec = pl.BlockSpec((N_CTX, TOK, HDIM), lambda i: (0, 0, 0))
    acc_spec = pl.BlockSpec((HDIM, FEATS), lambda i: (0, i))
    params = pltpu.CompilerParams(vmem_limit_bytes=24 << 20)
    first = pl.pallas_call(
        tiles_first_kernel,
        grid=(steps,),
        in_specs=[grad_spec, pl.BlockSpec((N_CTX, 1, TOK, FEATS), lambda i: (0, 0, 0, i))],
        out_specs=acc_spec,
        out_shape=jax.ShapeDtypeStruct((HDIM, N_CTX * HDIM), jnp.float32),
        scratch_shapes=[pltpu.VMEM((HDIM, LEN), jnp.bfloat16)],
        compiler_params=params,
        name="tiles0",
        cost_estimate=cost,
    )(grad0, gathered)
    return pl.pallas_call(
        tiles_second_kernel,
        grid=(steps,),
        in_specs=[
            pl.BlockSpec(memory_space=pltpu.SMEM),
            grad_spec,
            pl.BlockSpec((N_CTX, 1, TOK, FEATS), lambda i: (0, 1, 0, i)),
            acc_spec,
        ],
        out_specs=pl.BlockSpec((N_CTX, HDIM, HDIM), lambda i: (0, 0, 0)),
        out_shape=jax.ShapeDtypeStruct((N_CTX, HDIM, HDIM), jnp.bfloat16),
        scratch_shapes=[pltpu.VMEM((HDIM, LEN), jnp.bfloat16)],
        compiler_params=params,
        name="tiles1",
        cost_estimate=cost,
    )(lane, grad1, gathered, first)


def gram_kernel(tile_ref, left_ref, right_ref, new_left_ref, new_right_ref):
    for s in range(SPAN):
        tile_t = tile_ref[s] * (1.0 / math.sqrt(2 * N_DP * LEN))
        tile = jnp.transpose(tile_t)
        left = lax.dot(
            tile, tile_t, precision=lax.Precision.HIGHEST, preferred_element_type=jnp.float32
        )
        right = lax.dot(
            tile_t, tile, precision=lax.Precision.HIGHEST, preferred_element_type=jnp.float32
        )
        new_left_ref[0, 0, s] = BETA * left_ref[0, 0, s] + (1.0 - BETA) * left
        new_right_ref[0, 0, s] = BETA * right_ref[0, 0, s] + (1.0 - BETA) * right


def grams(tiles, left_old, right_old):
    vmem = pl.BlockSpec(memory_space=pltpu.VMEM)
    shape = jax.ShapeDtypeStruct(left_old.shape, jnp.float32)
    return pl.pallas_call(
        gram_kernel,
        in_specs=[vmem] * 3,
        out_specs=[vmem] * 2,
        out_shape=[shape, shape],
        name="grams",
        cost_estimate=pl.CostEstimate(
            flops=6 * 16 * HDIM**3, bytes_accessed=1 << 20, transcendentals=0
        ),
    )(tiles, left_old, right_old)


def swap(value, axes):
    return lax.all_to_all(value, axes, split_axis=0, concat_axis=0, tiled=True)


def owner_pairs():
    pairs = []
    for g in range(N_DP):
        for c in range(N_CTX):
            pairs.append((g * N_CTX + c, ((c // SPAN - g) % N_DP) * N_CTX + c))
    return pairs


def on_device(qkv_pre, d_out, inputs, conv_taps, left_old, right_old):
    gathered = lax.all_gather(inputs.reshape(2 * TOK, N_CTX * HDIM), PLANE, axis=0, tiled=True)
    gathered = gathered.reshape(N_CTX, 2, TOK, N_CTX * HDIM)

    received = [swap(pack(qkv_pre, d_out, seq), CTX) for seq in range(2)]
    gq, gkv = zip(*[attention(received[seq], conv_taps, seq) for seq in range(2)])
    gq = [swap(part, CTX) for part in gq]
    gkv = [swap(part, CTX) for part in gkv]
    grad_qkv = unpack(gq[0], gkv[0], gq[1], gkv[1])

    columns = [swap(part, PLANE) for part in gq]
    lane = (lax.axis_index("yl") * 2 + lax.axis_index("core")).astype(jnp.int32).reshape(1)
    partial = tile_sums(columns[0], columns[1], gathered, lane)
    arrived = swap(partial.reshape(N_Z, SPAN * HDIM, HDIM), "z")
    summed = jnp.sum(arrived.astype(jnp.float32), axis=0)
    tiles = lax.ppermute(summed, ALL, owner_pairs()).reshape(SPAN, HDIM, HDIM)
    new_left, new_right = grams(tiles, left_old, right_old)
    return (grad_qkv, new_left, new_right)


def solution(mesh):
    fine = Mesh(mesh.devices.reshape(4, 2, N_Z, 2, 2), ALL)
    tiles_spec = P(DP, CTX, None, None, None)
    return jax.shard_map(
        on_device,
        mesh=fine,
        in_specs=(
            P(None, DP, CTX, None),
            P(DP, CTX, None),
            P(DP, CTX, None),
            P(None, None, CTX),
            tiles_spec,
            tiles_spec,
        ),
        out_specs=(P(None, DP, CTX, None), tiles_spec, tiles_spec),
        check_vma=False,
    )
```

time: 695 us -> 320 us (0.46); the launches traced: 683 us -> 316 us
  waiting for transfers between devices: 306 us -> 121 us
  local copies, waits for them, and re-layouts: 118 us -> 4.6 us
  starting transfers between devices: 148 us -> 34.7 us
  blocking collectives: 0 us -> 83.2 us
  matrix products: 66.7 us -> 0 us
  Pallas kernels: 0 us -> 57.7 us
  other arithmetic: 28.6 us -> 0.15 us
    ppermute x10 -> x1, waiting for transfers between devices: 149 us -> 0.01 us  [on_device(): tiles = lax.ppermute(summed, ALL, owner_pairs()).reshape(SPAN, HDIM, HDIM)]
    ppermute x10 -> x1, starting transfers between devices: 120 us -> 5.03 us  [on_device(): tiles = lax.ppermute(summed, ALL, owner_pairs()).reshape(SPAN, HDIM, HDIM)]
    unnamed x2 -> x1, waiting for transfers between devices: 91 us -> 0.68 us
    all_to_all x0 -> x4, blocking collectives: none -> 83.2 us  [swap(): return lax.all_to_all(value, axes, split_axis=0, concat_axis=0, tiled=True)]
    pallas_call x0 -> x8, Pallas kernels: none -> 57.7 us  [the longest x2 23.5 us: attention(): pl.pallas_call(attention_kernel, in_specs=[vmem, vmem], out_specs=[vmem,...]
    all_to_all x4 -> x5, waiting for transfers between devices: 65.9 us -> 121 us  [swap(): return lax.all_to_all(value, axes, split_axis=0, concat_axis=0, tiled=True)]
    unnamed x65 -> x14, local copies, waits for them, and re-layouts: 58.5 us -> 4.6 us
    dot_general x20 -> x0, matrix products: 49.8 us -> none  [the longest x4 13.8 us: head_blocks(): jnp.einsum('pla,plm->pam', probability_halves, output_row_slab, preferred...]
  transfers between devices with their start and end apart: 15 -> 7, of which waited for: 8 -> 5; matrix products, arithmetic and copies ran while one was open for 28% -> 0% of each run, Pallas kernels for 0% -> 17%
where the time goes in v1:
time: 320 us; the launch traced here: 316 us
  waiting for transfers between devices  121 us (38%)
  blocking collectives  83.2 us (26%)
  Pallas kernels  57.7 us (18%)
  starting transfers between devices  34.7 us (11%)
  between operations  14.1 us (4%)
  local copies, waits for them, and re-layouts  4.6 us (1%)
    all_to_all x5, waiting for transfers between devices, swap(): return lax.all_to_all(value, axes, split_axis=0, concat_axis=0, tiled=True)  121 us
    all_to_all x4, blocking collectives, swap(): return lax.all_to_all(value, axes, split_axis=0, concat_axis=0, tiled=True)  83.2 us
    all_to_all x5, starting transfers between devices, swap(): return lax.all_to_all(value, axes, split_axis=0, concat_axis=0, tiled=True)  29.6 us
    pallas_call x2, Pallas kernels, attention(): pl.pallas_call(attention_kernel, in_specs=[vmem, vmem], out_specs=[vmem,...  23.5 us
    pallas_call x1, Pallas kernels, tile_sums(): pl.pallas_call(tiles_first_kernel, grid=(steps,), in_specs=[grad_spec, pl...  9.71 us
    pallas_call x1, Pallas kernels, tile_sums(): pl.pallas_call(tiles_second_kernel, grid=(steps,), in_specs=[pl.BlockSpec...  9.69 us
    pallas_call x2, Pallas kernels, pack(): pl.pallas_call(pack_kernel, grid=(N_CTX // width,), in_specs=[pl.BlockSpe...  7.75 us
  transfers between devices with their start and end apart: 7, of which 5 were waited for; matrix products, arithmetic and copies ran while one was open for 0% of the time, Pallas kernels for 17%

profile of v1, /device:TPU:46, one launch (start us, length us, event | category | flops | bytes accessed | tf_op | source)
XLA Modules:
  0.0 315.8 jit_solution(1095036732284817980)
XLA Ops:
  7.9 3.9 %pack0.1 = bf16[32,256,128]{2,1,0:T(8,128)(2,1)} custom-call(bf16[3,2,64,4096]{3,2,1,0:T(8,128)(2,1)} %qkv_ref.3, bf16[2,64,4096]{2,1,0:T(8,128)(2,1)} %dout_ref.3), custom_call_target="tpu_custom_call" | custom-call | bytes 4194304 | tf_op jit(solution)/shard_map/pack0/pallas_call | solution.py:45
  11.8 9.6 %all-to-all-start = ((bf16[32,256,128]{2,1,0:T(8,128)(2,1)}), bf16[32,256,128]{2,1,0:T(8,128)(2,1)S(1)}, u32[]{:S(2)}, u32[]{:S(2)}) async-start(bf16[32,256,128]{2,1,0:T(8,128)(2,1)} %pack0.1), calls=%async_computation | async-start | bytes 4194304 | tf_op jit(solution)/shard_map/all_to_all | solution.py:278
  21.4 3.9 %pack1.1 = bf16[32,256,128]{2,1,0:T(8,128)(2,1)} custom-call(bf16[3,2,64,4096]{3,2,1,0:T(8,128)(2,1)} %qkv_ref.3, bf16[2,64,4096]{2,1,0:T(8,128)(2,1)} %dout_ref.3), custom_call_target="tpu_custom_call" | custom-call | bytes 4194304 | tf_op jit(solution)/shard_map/pack1/pallas_call | solution.py:45
  25.3 46.7 %all-to-all-done.recv_ref = bf16[32,256,128]{2,1,0:T(8,128)(2,1)S(1)} async-done(((bf16[32,256,128]{2,1,0:T(8,128)(2,1)}), bf16[32,256,128]{2,1,0:T(8,128)(2,1)S(1)}, u32[]{:S(2)}, u32[]{:S(2)}) %all-to-all-start) | async-done | bytes 2097184 | tf_op jit(solution)/shard_map/all_to_all | solution.py:278
  73.3 4.4 %all-to-all-start.3 = ((bf16[32,256,128]{2,1,0:T(8,128)(2,1)}), bf16[32,256,128]{2,1,0:T(8,128)(2,1)S(1)}, u32[]{:S(2)}, u32[]{:S(2)}) async-start(bf16[32,256,128]{2,1,0:T(8,128)(2,1)} %pack1.1), calls=%async_computation.3 | async-start | bytes 4194304 | tf_op jit(solution)/shard_map/all_to_all | solution.py:278
  77.7 1.6 copy-done.1
  79.3 11.8 %attention0.1 = (bf16[32,64,128]{2,1,0:T(8,128)(2,1)}, bf16[32,128,128]{2,1,0:T(8,128)(2,1)}) custom-call(bf16[32,256,128]{2,1,0:T(8,128)(2,1)S(1)} %copy-done.1, f32[3,3,128]{2,1,0:T(4,128)S(1)} %copy-done.2), custom_call_target="tpu_custom_call" | custom-call | flops 3221225472 | bytes 4194304 | tf_op jit(solution)/shard_map/attention0/pallas_call | solution.py:134
  91.0 37.1 %all-to-all-done.3.recv_ref = bf16[32,256,128]{2,1,0:T(8,128)(2,1)S(1)} async-done(((bf16[32,256,128]{2,1,0:T(8,128)(2,1)}), bf16[32,256,128]{2,1,0:T(8,128)(2,1)S(1)}, u32[]{:S(2)}, u32[]{:S(2)}) %all-to-all-start.3) | async-done | bytes 2097184 | tf_op jit(solution)/shard_map/all_to_all | solution.py:278
  128.2 4.4 %all-to-all-start.1 = ((bf16[32,64,128]{2,1,0:T(8,128)(2,1)}), bf16[32,64,128]{2,1,0:T(8,128)(2,1)S(1)}, u32[]{:S(2)}, u32[]{:S(2)}) async-start(bf16[32,64,128]{2,1,0:T(8,128)(2,1)} %get-tuple-element.9), calls=%async_computation.1 | async-start | bytes 1048576 | tf_op jit(solution)/shard_map/all_to_all | solution.py:278
  132.6 11.7 %attention1.1 = (bf16[32,64,128]{2,1,0:T(8,128)(2,1)S(1)}, bf16[32,128,128]{2,1,0:T(8,128)(2,1)}) custom-call(bf16[32,256,128]{2,1,0:T(8,128)(2,1)S(1)} %all-to-all-done.3.recv_ref, f32[3,3,128]{2,1,0:T(4,128)S(1)} %copy-done.2), custom_call_target="tpu_custom_call" | custom-call | flops 3221225472 | bytes 4194304 | tf_op jit(solution)/shard_map/attention1/pallas_call | solution.py:134
  144.3 5.1 %all-to-all-done.1.q0_ref = bf16[32,64,128]{2,1,0:T(8,128)(2,1)S(1)} async-done(((bf16[32,64,128]{2,1,0:T(8,128)(2,1)}), bf16[32,64,128]{2,1,0:T(8,128)(2,1)S(1)}, u32[]{:S(2)}, u32[]{:S(2)}) %all-to-all-start.1) | async-done | bytes 524320 | tf_op jit(solution)/shard_map/all_to_all | solution.py:278
  149.4 21.0 %all_to_all.45.q1_ref = bf16[32,64,128]{2,1,0:T(8,128)(2,1)S(1)} all-to-all(bf16[32,64,128]{2,1,0:T(8,128)(2,1)S(1)} %get-tuple-element.11), channel_id=1, replica_groups=mesh['x'=4,'yh'=2,'z'=8,'yl'=2,'core'=2] {'z','yl','core'}, dimensions={0} | all-to-all | bytes 1048576 | tf_op jit(solution)/shard_map/all_to_all | solution.py:278
  170.4 15.6 %all_to_all.46.grad_ref = bf16[32,64,128]{2,1,0:T(8,128)(2,1)S(1)} all-to-all(bf16[32,64,128]{2,1,0:T(8,128)(2,1)S(1)} %all_to_all.45.q1_ref), channel_id=1, replica_groups=mesh['x'=4,'yh'=2,'z'=8,'yl'=2,'core'=2] {'x','yh','yl','core'}, dimensions={0} | all-to-all | bytes 1048576 | tf_op jit(solution)/shard_map/all_to_all | solution.py:278
  186.0 15.0 %all_to_all.47.grad_ref = bf16[32,64,128]{2,1,0:T(8,128)(2,1)S(1)} all-to-all(bf16[32,64,128]{2,1,0:T(8,128)(2,1)S(1)} %all-to-all-done.1.q0_ref), channel_id=1, replica_groups=mesh['x'=4,'yh'=2,'z'=8,'yl'=2,'core'=2] {'x','yh','yl','core'}, dimensions={0} | all-to-all | bytes 1048576 | tf_op jit(solution)/shard_map/all_to_all | solution.py:278
  201.0 6.5 %all-to-all-start.2 = ((bf16[32,128,128]{2,1,0:T(8,128)(2,1)}), bf16[32,128,128]{2,1,0:T(8,128)(2,1)}, u32[]{:S(2)}, u32[]{:S(2)}) async-start(bf16[32,128,128]{2,1,0:T(8,128)(2,1)} %get-tuple-element.10), calls=%async_computation.2 | async-start | bytes 2097152 | tf_op jit(solution)/shard_map/all_to_all | solution.py:278
  207.6 9.7 %tiles0.1.first_ref = f32[128,4096]{1,0:T(8,128)S(1)} custom-call(bf16[32,64,128]{2,1,0:T(8,128)(2,1)S(1)} %all_to_all.47.grad_ref, bf16[32,2,64,4096]{3,2,1,0:T(8,128)(2,1)} %bitcast.6), custom_call_target="tpu_custom_call" | custom-call | flops 2147483648 | bytes 20971520 | tf_op jit(solution)/shard_map/tiles0/pallas_call | solution.py:219
  217.3 9.7 %tiles1.1 = bf16[32,128,128]{2,1,0:T(8,128)(2,1)S(1)} custom-call(s32[1]{0:T(128)} %bitcast.lane_ref, bf16[32,64,128]{2,1,0:T(8,128)(2,1)S(1)} %all_to_all.46.grad_ref, bf16[32,2,64,4096]{3,2,1,0:T(8,128)(2,1)} %bitcast.7, f32[128,4096]{1,0:T(8,128)S(1)} %tiles0.1.first_ref), custom_call_target="tpu_custom_call" | custom-call | flops 2147483648 | bytes 20971520 | tf_op jit(solution)/shard_map/tiles1/pallas_call | solution.py:230
  227.0 8.7 %all-to-all-done.2.kv0_ref = bf16[32,128,128]{2,1,0:T(8,128)(2,1)} async-done(((bf16[32,128,128]{2,1,0:T(8,128)(2,1)}), bf16[32,128,128]{2,1,0:T(8,128)(2,1)}, u32[]{:S(2)}, u32[]{:S(2)}) %all-to-all-start.2) | async-done | bytes 1048608 | tf_op jit(solution)/shard_map/all_to_all | solution.py:278
  235.8 31.6 %all_to_all.48 = bf16[8,512,128]{2,1,0:T(8,128)(2,1)S(1)} all-to-all(bf16[8,512,128]{2,1,0:T(8,128)(2,1)S(1)} %bitcast.5), channel_id=1, replica_groups=mesh['x'=4,'yh'=2,'z'=8,'yl'=2,'core'=2] {'z'}, dimensions={0} | all-to-all | bytes 2097152 | tf_op jit(solution)/shard_map/all_to_all | solution.py:278
  267.4 4.7 %all-to-all-start.5 = ((bf16[32,128,128]{2,1,0:T(8,128)(2,1)}), bf16[32,128,128]{2,1,0:T(8,128)(2,1)S(1)}, u32[]{:S(2)}, u32[]{:S(2)}) async-start(bf16[32,128,128]{2,1,0:T(8,128)(2,1)} %get-tuple-element.12), calls=%async_computation.5 | async-start | bytes 2097152 | tf_op jit(solution)/shard_map/all_to_all | solution.py:278
  272.2 5.0 %collective-permute-start = (f32[512,128]{1,0:T(8,128)S(1)}, f32[512,128]{1,0:T(8,128)S(1)}, u32[]{:S(2)}, u32[]{:S(2)}) collective-permute-start(f32[512,128]{1,0:T(8,128)S(1)} %convert_reduce_fusion), channel_id=1, source_target_pairs={{0,0},{1,1},{2,2},{3,3},{4,36},{5,37},{6,38},{7,39},{8,72},{9,73},... | collective-permute-start | bytes 786440 | tf_op jit(solution)/shard_map/ppermute | solution.py:304
  277.2 23.0 %all-to-all-done.5.kv1_ref = bf16[32,128,128]{2,1,0:T(8,128)(2,1)S(1)} async-done(((bf16[32,128,128]{2,1,0:T(8,128)(2,1)}), bf16[32,128,128]{2,1,0:T(8,128)(2,1)S(1)}, u32[]{:S(2)}, u32[]{:S(2)}) %all-to-all-start.5) | async-done | bytes 1048608 | tf_op jit(solution)/shard_map/all_to_all | solution.py:278
  301.2 4.5 %unpack.1 = bf16[3,2,64,4096]{3,2,1,0:T(8,128)(2,1)} custom-call(bf16[32,64,128]{2,1,0:T(8,128)(2,1)} %copy-done.3, bf16[32,128,128]{2,1,0:T(8,128)(2,1)} %all-to-all-done.2.kv0_ref, bf16[32,64,128]{2,1,0:T(8,128)(2,1)} %copy-done.4, bf16[32,128,128]{2,1,0:T(8,128)(2,1)} %copy-done.5), custom_call_target="tpu_custom_call" | custom-call | bytes 6291456 | tf_op jit(solution)/shard_map/unpack/pallas_call | solution.py:170
  306.4 2.5 grams.1
  (18 shorter events, 3.9 us)
Async XLA Ops:
  7.2 200.4 %all-gather.2.cloned.1.call-start = ((), (), s32[]{:S(2)}) async-start(), calls=%async_computation.9 | async-start | bytes 34603008 | tf_op jit(solution)/shard_map/all_gather | solution.py:290
  11.8 60.2 %all-to-all-start = ((bf16[32,256,128]{2,1,0:T(8,128)(2,1)}), bf16[32,256,128]{2,1,0:T(8,128)(2,1)S(1)}, u32[]{:S(2)}, u32[]{:S(2)}) async-start(bf16[32,256,128]{2,1,0:T(8,128)(2,1)} %pack0.1), calls=%async_computation | async-start | bytes 4194304 | tf_op jit(solution)/shard_map/all_to_all | solution.py:278
  25.3 52.4 %copy-start.2 = (f32[3,3,128]{2,1,0:T(4,128)S(1)}, f32[3,3,128]{2,1,0:T(4,128)}, u32[]{:S(2)}) copy-start(f32[3,3,128]{2,1,0:T(4,128)} %taps_ref.3) | copy-start | bytes 13828
  71.9 1.3 copy-start
  73.3 54.9 %all-to-all-start.3 = ((bf16[32,256,128]{2,1,0:T(8,128)(2,1)}), bf16[32,256,128]{2,1,0:T(8,128)(2,1)S(1)}, u32[]{:S(2)}, u32[]{:S(2)}) async-start(bf16[32,256,128]{2,1,0:T(8,128)(2,1)} %pack1.1), calls=%async_computation.3 | async-start | bytes 4194304 | tf_op jit(solution)/shard_map/all_to_all | solution.py:278
  77.7 1.6 copy-start.1
  128.2 21.2 %all-to-all-start.1 = ((bf16[32,64,128]{2,1,0:T(8,128)(2,1)}), bf16[32,64,128]{2,1,0:T(8,128)(2,1)S(1)}, u32[]{:S(2)}, u32[]{:S(2)}) async-start(bf16[32,64,128]{2,1,0:T(8,128)(2,1)} %get-tuple-element.9), calls=%async_computation.1 | async-start | bytes 1048576 | tf_op jit(solution)/shard_map/all_to_all | solution.py:278
  149.4 51.6 %copy-start.3 = (bf16[32,64,128]{2,1,0:T(8,128)(2,1)}, bf16[32,64,128]{2,1,0:T(8,128)(2,1)S(1)}, u32[]{:S(2)}) copy-start(bf16[32,64,128]{2,1,0:T(8,128)(2,1)S(1)} %all-to-all-done.1.q0_ref) | copy-start | bytes 1572868
  170.4 30.6 %copy-start.4 = (bf16[32,64,128]{2,1,0:T(8,128)(2,1)}, bf16[32,64,128]{2,1,0:T(8,128)(2,1)S(1)}, u32[]{:S(2)}) copy-start(bf16[32,64,128]{2,1,0:T(8,128)(2,1)S(1)} %all_to_all.45.q1_ref) | copy-start | bytes 1572868
  201.0 34.7 %all-to-all-start.2 = ((bf16[32,128,128]{2,1,0:T(8,128)(2,1)}), bf16[32,128,128]{2,1,0:T(8,128)(2,1)}, u32[]{:S(2)}, u32[]{:S(2)}) async-start(bf16[32,128,128]{2,1,0:T(8,128)(2,1)} %get-tuple-element.10), calls=%async_computation.2 | async-start | bytes 2097152 | tf_op jit(solution)/shard_map/all_to_all | solution.py:278
  267.4 32.8 %all-to-all-start.5 = ((bf16[32,128,128]{2,1,0:T(8,128)(2,1)}), bf16[32,128,128]{2,1,0:T(8,128)(2,1)S(1)}, u32[]{:S(2)}, u32[]{:S(2)}) async-start(bf16[32,128,128]{2,1,0:T(8,128)(2,1)} %get-tuple-element.12), calls=%async_computation.5 | async-start | bytes 2097152 | tf_op jit(solution)/shard_map/all_to_all | solution.py:278
  272.2 33.5 %collective-permute-start = (f32[512,128]{1,0:T(8,128)S(1)}, f32[512,128]{1,0:T(8,128)S(1)}, u32[]{:S(2)}, u32[]{:S(2)}) collective-permute-start(f32[512,128]{1,0:T(8,128)S(1)} %convert_reduce_fusion), channel_id=1, source_target_pairs={{0,0},{1,1},{2,2},{3,3},{4,36},{5,37},{6,38},{7,39},{8,72},{9,73},... | collective-permute-start | bytes 786440 | tf_op jit(solution)/shard_map/ppermute | solution.py:304
  300.2 1.0 copy-start.5
  305.7 0.7 copy-start.6
Sparse Core Ops, SparseCore 0:
  10.6 169.8 all-gather.1

commit v2 on v1

--- a/solution.py
+++ b/solution.py
@@ -22,6 +22,7 @@
 LEN = N_CTX * TOK
 BLOCK = 256
 PAD = 8
+VMEM = 60 << 20
 
 
 def nt_dot(a, b):
@@ -41,7 +42,7 @@
         out_ref[c, 3 * TOK : 4 * TOK, :] = dout_ref[0, :, lanes]
 
 
-def pack(qkv_pre, d_out, seq, width=8):
+def pack(qkv_pre, d_out, seq, width=16):
     return pl.pallas_call(
         pack_kernel,
         grid=(N_CTX // width,),
@@ -51,14 +52,14 @@
         ],
         out_specs=pl.BlockSpec((width, 4 * TOK, HDIM), lambda i: (i, 0, 0)),
         out_shape=jax.ShapeDtypeStruct((N_CTX, 4 * TOK, HDIM), jnp.bfloat16),
+        compiler_params=pltpu.CompilerParams(vmem_limit_bytes=VMEM),
         name=f"pack{seq}",
         cost_estimate=pl.CostEstimate(flops=0, bytes_accessed=4 << 20, transcendentals=0),
     )(qkv_pre, d_out)
 
 
-def attention_kernel(
-    recv_ref, taps_ref, gq_ref, gkv_ref, pad_ref, post_ref, kt_ref, s_ref, w_ref, grad_ref
-):
+def attention_kernel(group_ref, recv_ref, taps_ref, back_ref, *rest):
+    column_refs, (pad_ref, post_ref, kt_ref, s_ref, w_ref, grad_ref) = rest[:N_Z], rest[N_Z:]
     scale = 1.0 / math.sqrt(HDIM)
     factor = scale * math.log2(math.e)
     pad_ref[0:PAD, :] = jnp.zeros((PAD, HDIM), jnp.float32)
@@ -122,23 +123,22 @@
             + taps_ref[j, 1:2, :] * (grad_ref[j, 1 : LEN + 1, :] * factor_back)
             + taps_ref[j, 2:3, :] * (grad_ref[j, 2 : LEN + 2, :] * factor_back)
         )
-        halves = grads.astype(jnp.bfloat16).reshape(N_CTX, TOK, HDIM)
-        if j == 0:
-            gq_ref[...] = halves
-        else:
-            gkv_ref[:, (j - 1) * TOK : j * TOK, :] = halves
-
-
-def attention(received, taps, seq):
+        back_ref[:, j * TOK : (j + 1) * TOK, :] = grads.astype(jnp.bfloat16).reshape(
+            N_CTX, TOK, HDIM
+        )
+    for k in range(N_Z):
+        first = ((group_ref[0] + k) & (N_Z - 1)) * SPAN
+        column_refs[k][...] = back_ref[pl.ds(first, SPAN), 0:TOK, :]
+
+
+def attention(received, taps, group, seq):
     vmem = pl.BlockSpec(memory_space=pltpu.VMEM)
-    return pl.pallas_call(
+    results = pl.pallas_call(
         attention_kernel,
-        in_specs=[vmem, vmem],
-        out_specs=[vmem, vmem],
-        out_shape=[
-            jax.ShapeDtypeStruct((N_CTX, TOK, HDIM), jnp.bfloat16),
-            jax.ShapeDtypeStruct((N_CTX, 2 * TOK, HDIM), jnp.bfloat16),
-        ],
+        in_specs=[pl.BlockSpec(memory_space=pltpu.SMEM), vmem, vmem],
+        out_specs=[vmem] * (1 + N_Z),
+        out_shape=[jax.ShapeDtypeStruct((N_CTX, 3 * TOK, HDIM), jnp.bfloat16)]
+        + [jax.ShapeDtypeStruct((SPAN, TOK, HDIM), jnp.bfloat16)] * N_Z,
         scratch_shapes=[
             pltpu.VMEM((LEN + PAD, HDIM), jnp.float32),
             pltpu.VMEM((3, LEN, HDIM), jnp.bfloat16),
@@ -147,107 +147,90 @@
             pltpu.VMEM((LEN, BLOCK), jnp.float32),
             pltpu.VMEM((3, LEN + PAD, HDIM), jnp.float32),
         ],
-        compiler_params=pltpu.CompilerParams(vmem_limit_bytes=32 << 20),
+        compiler_params=pltpu.CompilerParams(vmem_limit_bytes=VMEM),
         name=f"attention{seq}",
         cost_estimate=pl.CostEstimate(
             flops=6 * LEN * LEN * HDIM, bytes_accessed=4 << 20, transcendentals=LEN * LEN // 2
         ),
-    )(received, taps)
-
-
-def unpack_kernel(q0_ref, kv0_ref, q1_ref, kv1_ref, out_ref):
-    for c in range(q0_ref.shape[0]):
+    )(group, received, taps)
+    return results[0], results[1:]
+
+
+def unpack_kernel(first_ref, second_ref, out_ref):
+    for c in range(first_ref.shape[0]):
         lanes = slice(c * HDIM, (c + 1) * HDIM)
-        for seq, (q_ref, kv_ref) in enumerate(((q0_ref, kv0_ref), (q1_ref, kv1_ref))):
-            out_ref[0, seq, :, lanes] = q_ref[c]
-            out_ref[1, seq, :, lanes] = kv_ref[c, 0:TOK, :]
-            out_ref[2, seq, :, lanes] = kv_ref[c, TOK : 2 * TOK, :]
-
-
-def unpack(q0, kv0, q1, kv1, width=8):
-    q_spec = pl.BlockSpec((width, TOK, HDIM), lambda i: (i, 0, 0))
-    kv_spec = pl.BlockSpec((width, 2 * TOK, HDIM), lambda i: (i, 0, 0))
+        for seq, ref in enumerate((first_ref, second_ref)):
+            for j in range(3):
+                out_ref[j, seq, :, lanes] = ref[c, j * TOK : (j + 1) * TOK, :]
+
+
+def unpack(first, second, width=16):
+    spec = pl.BlockSpec((width, 3 * TOK, HDIM), lambda i: (i, 0, 0))
     return pl.pallas_call(
         unpack_kernel,
         grid=(N_CTX // width,),
-        in_specs=[q_spec, kv_spec, q_spec, kv_spec],
+        in_specs=[spec, spec],
         out_specs=pl.BlockSpec((3, 2, TOK, width * HDIM), lambda i: (0, 0, 0, i)),
         out_shape=jax.ShapeDtypeStruct((3, 2, TOK, N_CTX * HDIM), jnp.bfloat16),
+        compiler_params=pltpu.CompilerParams(vmem_limit_bytes=VMEM),
         name="unpack",
         cost_estimate=pl.CostEstimate(flops=0, bytes_accessed=6 << 20, transcendentals=0),
-    )(q0, kv0, q1, kv1)
+    )(first, second)
 
 
 FEATS = 512
 
 
-def tiles_first_kernel(grad_ref, x_ref, out_ref, gt_ref):
-    @pl.when(pl.program_id(0) == 0)
-    def _():
-        full = grad_ref[...].reshape(LEN, HDIM).astype(jnp.float32)
-        gt_ref[...] = jnp.transpose(full).astype(jnp.bfloat16)
-
-    out_ref[...] = nn_dot(gt_ref[...], x_ref[:, 0].reshape(LEN, FEATS))
-
-
-def tiles_second_kernel(lane_ref, grad_ref, x_ref, first_ref, out_ref, gt_ref):
+def tiles_kernel(where_ref, x_ref, *rest):
+    column_refs, (out_ref, all_ref, gt_ref) = rest[: 2 * N_DP], rest[2 * N_DP :]
     step = pl.program_id(0)
 
     @pl.when(step == 0)
     def _():
-        full = grad_ref[...].reshape(LEN, HDIM).astype(jnp.float32)
+        for k in range(N_DP):
+            first = ((where_ref[0] - k + N_DP) & (N_DP - 1)) * SPAN
+            for seq in range(2):
+                all_ref[pl.ds(first, SPAN), seq * TOK : (seq + 1) * TOK, :] = column_refs[
+                    seq * N_DP + k
+                ][...]
+        full = all_ref[...].reshape(2 * LEN, HDIM).astype(jnp.float32)
         gt_ref[...] = jnp.transpose(full).astype(jnp.bfloat16)
 
-    done = (first_ref[...] + nn_dot(gt_ref[...], x_ref[:, 0].reshape(LEN, FEATS))).astype(
-        jnp.bfloat16
-    )
+    done = nn_dot(gt_ref[...], x_ref[...].reshape(2 * LEN, FEATS)).astype(jnp.bfloat16)
     for k in range(FEATS // HDIM):
-        ahead = (step * (FEATS // HDIM) + k - lane_ref[0] + N_CTX) & (N_CTX - 1)
+        ahead = (step * (FEATS // HDIM) + k - where_ref[1] + N_CTX) & (N_CTX - 1)
         offset = (SPAN - (ahead & (SPAN - 1))) & (SPAN - 1)
         plane = ((ahead + SPAN - 1) // SPAN) & (N_Z - 1)
         out_ref[plane * SPAN + offset] = done[:, k * HDIM : (k + 1) * HDIM]
 
 
-def tile_sums(grad0, grad1, gathered, lane):
-    steps = N_CTX * HDIM // FEATS
-    cost = pl.CostEstimate(
-        flops=2 * LEN * HDIM * HDIM * N_CTX, bytes_accessed=20 << 20, transcendentals=0
-    )
-    grad_spec = pl.BlockSpec((N_CTX, TOK, HDIM), lambda i: (0, 0, 0))
-    acc_spec = pl.BlockSpec((HDIM, FEATS), lambda i: (0, i))
-    params = pltpu.CompilerParams(vmem_limit_bytes=24 << 20)
-    first = pl.pallas_call(
-        tiles_first_kernel,
-        grid=(steps,),
-        in_specs=[grad_spec, pl.BlockSpec((N_CTX, 1, TOK, FEATS), lambda i: (0, 0, 0, i))],
-        out_specs=acc_spec,
-        out_shape=jax.ShapeDtypeStruct((HDIM, N_CTX * HDIM), jnp.float32),
-        scratch_shapes=[pltpu.VMEM((HDIM, LEN), jnp.bfloat16)],
-        compiler_params=params,
-        name="tiles0",
-        cost_estimate=cost,
-    )(grad0, gathered)
+def tile_sums(columns, gathered, where):
+    column_spec = pl.BlockSpec((SPAN, TOK, HDIM), lambda i: (0, 0, 0))
     return pl.pallas_call(
-        tiles_second_kernel,
-        grid=(steps,),
+        tiles_kernel,
+        grid=(N_CTX * HDIM // FEATS,),
         in_specs=[
             pl.BlockSpec(memory_space=pltpu.SMEM),
-            grad_spec,
-            pl.BlockSpec((N_CTX, 1, TOK, FEATS), lambda i: (0, 1, 0, i)),
-            acc_spec,
-        ],
+            pl.BlockSpec((N_CTX, 2 * TOK, FEATS), lambda i: (0, 0, i)),
+        ]
+        + [column_spec] * (2 * N_DP),
         out_specs=pl.BlockSpec((N_CTX, HDIM, HDIM), lambda i: (0, 0, 0)),
         out_shape=jax.ShapeDtypeStruct((N_CTX, HDIM, HDIM), jnp.bfloat16),
-        scratch_shapes=[pltpu.VMEM((HDIM, LEN), jnp.bfloat16)],
-        compiler_params=params,
-        name="tiles1",
-        cost_estimate=cost,
-    )(lane, grad1, gathered, first)
+        scratch_shapes=[
+            pltpu.VMEM((N_CTX, 2 * TOK, HDIM), jnp.bfloat16),
+            pltpu.VMEM((HDIM, 2 * LEN), jnp.bfloat16),
+        ],
+        compiler_params=pltpu.CompilerParams(vmem_limit_bytes=VMEM),
+        name="tiles",
+        cost_estimate=pl.CostEstimate(
+            flops=4 * LEN * HDIM * HDIM * N_CTX, bytes_accessed=34 << 20, transcendentals=0
+        ),
+    )(where, gathered, *columns)
 
 
 def gram_kernel(tile_ref, left_ref, right_ref, new_left_ref, new_right_ref):
     for s in range(SPAN):
-        tile_t = tile_ref[s] * (1.0 / math.sqrt(2 * N_DP * LEN))
+        tile_t = tile_ref[s].astype(jnp.float32) * (1.0 / math.sqrt(2 * N_DP * LEN))
         tile = jnp.transpose(tile_t)
         left = lax.dot(
             tile, tile_t, precision=lax.Precision.HIGHEST, preferred_element_type=jnp.float32
@@ -286,21 +269,35 @@
     return pairs
 
 
+def column_pairs(k):
+    pairs = []
+    for g in range(N_DP):
+        for c in range(N_CTX):
+            z, lane = c // SPAN, c % SPAN
+            pairs.append((g * N_CTX + c, z * N_CTX + (g + k) % N_Z * SPAN + lane))
+    return pairs
+
+
 def on_device(qkv_pre, d_out, inputs, conv_taps, left_old, right_old):
+    group = (lax.axis_index("x") * 2 + lax.axis_index("yh")).astype(jnp.int32)
+    plane = lax.axis_index("z").astype(jnp.int32)
+    lane = (lax.axis_index("yl") * 2 + lax.axis_index("core")).astype(jnp.int32)
+
     gathered = lax.all_gather(inputs.reshape(2 * TOK, N_CTX * HDIM), PLANE, axis=0, tiled=True)
-    gathered = gathered.reshape(N_CTX, 2, TOK, N_CTX * HDIM)
+    gathered = gathered.reshape(N_CTX, 2 * TOK, N_CTX * HDIM)
 
     received = [swap(pack(qkv_pre, d_out, seq), CTX) for seq in range(2)]
-    gq, gkv = zip(*[attention(received[seq], conv_taps, seq) for seq in range(2)])
-    gq = [swap(part, CTX) for part in gq]
-    gkv = [swap(part, CTX) for part in gkv]
-    grad_qkv = unpack(gq[0], gkv[0], gq[1], gkv[1])
-
-    columns = [swap(part, PLANE) for part in gq]
-    lane = (lax.axis_index("yl") * 2 + lax.axis_index("core")).astype(jnp.int32).reshape(1)
-    partial = tile_sums(columns[0], columns[1], gathered, lane)
-    arrived = swap(partial.reshape(N_Z, SPAN * HDIM, HDIM), "z")
-    summed = jnp.sum(arrived.astype(jnp.float32), axis=0)
+    returned, columns = [], []
+    for seq in range(2):
+        back, parts = attention(received[seq], conv_taps, group.reshape(1), seq)
+        columns += [lax.ppermute(part, ALL, column_pairs(k)) for k, part in enumerate(parts)]
+        returned.append(swap(back, CTX))
+    grad_qkv = unpack(returned[0], returned[1])
+
+    partial = tile_sums(columns, gathered, jnp.stack([plane, lane]))
+    summed = lax.psum_scatter(
+        partial.reshape(N_Z, SPAN * HDIM, HDIM), "z", scatter_dimension=0, tiled=True
+    )[0]
     tiles = lax.ppermute(summed, ALL, owner_pairs()).reshape(SPAN, HDIM, HDIM)
     new_left, new_right = grams(tiles, left_old, right_old)
     return (grad_qkv, new_left, new_right)

time: 320 us -> 341 us (1.066)
  blocking collectives: 83.2 us -> 0 us
  waiting for transfers between devices: 121 us -> 185 us
  starting transfers between devices: 34.7 us -> 80.6 us
    all_to_all x4 -> x0, blocking collectives: 83.2 us -> none  [swap(): return lax.all_to_all(value, axes, split_axis=0, concat_axis=0, tiled=True)]
    ppermute x0 -> x16, starting transfers between devices: none -> 52.6 us  [on_device(): lax.ppermute(part, ALL, column_pairs(k))]
    reduce_scatter x0 -> x1, waiting for transfers between devices: none -> 38.4 us  [on_device(): lax.psum_scatter(partial.reshape(N_Z, SPAN * HDIM, HDIM), 'z', scatter_di...]
    ppermute x0 -> x16, waiting for transfers between devices: none -> 35 us  [on_device(): lax.ppermute(part, ALL, column_pairs(k))]
    all_to_all x5 -> x4, waiting for transfers between devices: 121 us -> 110 us  [swap(): return lax.all_to_all(value, axes, split_axis=0, concat_axis=0, tiled=True)]
    all_to_all x5 -> x4, starting transfers between devices: 29.6 us -> 22.9 us  [swap(): return lax.all_to_all(value, axes, split_axis=0, concat_axis=0, tiled=True)]
    pallas_call x5 -> x4, Pallas kernels: 47.4 us -> 46.7 us  [the longest x2 27.9 us: attention(): pl.pallas_call(attention_kernel, in_specs=[pl.BlockSpec(memory_space=pltp...]
  transfers between devices with their start and end apart: 7 -> 23, of which waited for: 5 -> 10; matrix products, arithmetic and copies ran while one was open for 0% -> 0% of each run, Pallas kernels for 17% -> 15%
where the time goes in v2:
time: 341 us; the launch traced here: 340 us
  waiting for transfers between devices  185 us (54%)
  starting transfers between devices  80.6 us (24%)
  Pallas kernels  54.7 us (16%)
  between operations  14.3 us (4%)
  local copies, waits for them, and re-layouts  4.48 us (1%)
    all_to_all x4, waiting for transfers between devices, swap(): return lax.all_to_all(value, axes, split_axis=0, concat_axis=0, tiled=True)  110 us
    ppermute x16, starting transfers between devices, on_device(): lax.ppermute(part, ALL, column_pairs(k))  52.6 us
    reduce_scatter x1, waiting for transfers between devices, on_device(): lax.psum_scatter(partial.reshape(N_Z, SPAN * HDIM, HDIM), 'z', scatter_di...  38.4 us
    ppermute x16, waiting for transfers between devices, on_device(): lax.ppermute(part, ALL, column_pairs(k))  35 us
    pallas_call x2, Pallas kernels, attention(): pl.pallas_call(attention_kernel, in_specs=[pl.BlockSpec(memory_space=pltp...  27.9 us
    all_to_all x4, starting transfers between devices, swap(): return lax.all_to_all(value, axes, split_axis=0, concat_axis=0, tiled=True)  22.9 us
    pallas_call x1, Pallas kernels, tile_sums(): pl.pallas_call(tiles_kernel, grid=(N_CTX * HDIM // FEATS,), in_specs=[pl....  15.4 us
  transfers between devices with their start and end apart: 23, of which 10 were waited for; matrix products, arithmetic and copies ran while one was open for 0% of the time, Pallas kernels for 15%

profile of v2, /device:TPU:46, one launch (start us, length us, event | category | flops | bytes accessed | tf_op | source)
XLA Modules:
  0.0 339.8 jit_solution(6359864631904202277)
XLA Ops:
  10.6 9.6 %all-to-all-start = ((bf16[32,256,128]{2,1,0:T(8,128)(2,1)}), bf16[32,256,128]{2,1,0:T(8,128)(2,1)S(1)}, u32[]{:S(2)}, u32[]{:S(2)}) async-start(bf16[32,256,128]{2,1,0:T(8,128)(2,1)} %pack0.1), calls=%async_computation | async-start | bytes 4194304 | tf_op jit(solution)/shard_map/all_to_all | solution.py:261
  23.0 47.8 %all-to-all-done.recv_ref = bf16[32,256,128]{2,1,0:T(8,128)(2,1)S(1)} async-done(((bf16[32,256,128]{2,1,0:T(8,128)(2,1)}), bf16[32,256,128]{2,1,0:T(8,128)(2,1)S(1)}, u32[]{:S(2)}, u32[]{:S(2)}) %all-to-all-start) | async-done | bytes 2097184 | tf_op jit(solution)/shard_map/all_to_all | solution.py:261
  72.1 4.4 %all-to-all-start.2 = ((bf16[32,256,128]{2,1,0:T(8,128)(2,1)}), bf16[32,256,128]{2,1,0:T(8,128)(2,1)S(1)}, u32[]{:S(2)}, u32[]{:S(2)}) async-start(bf16[32,256,128]{2,1,0:T(8,128)(2,1)} %pack1.1), calls=%async_computation.2 | async-start | bytes 4194304 | tf_op jit(solution)/shard_map/all_to_all | solution.py:261
  76.5 14.0 %attention0.1 = (bf16[32,192,128]{2,1,0:T(8,128)(2,1)}, bf16[4,64,128]{2,1,0:T(8,128)(2,1)}, bf16[4,64,128]{2,1,0:T(8,128)(2,1)}, bf16[4,64,128]{2,1,0:T(8,128)(...) custom-call(s32[1]{0:T(128)} %bitcast.group_ref, ...), custom_call_target="tpu_custom_call" | custom-call | flops 3221225472 | bytes 4194304 | tf_op jit(solution)/shard_map/attention0/pallas_call | solution.py:136
  90.5 36.5 %all-to-all-done.2.recv_ref = bf16[32,256,128]{2,1,0:T(8,128)(2,1)S(1)} async-done(((bf16[32,256,128]{2,1,0:T(8,128)(2,1)}), bf16[32,256,128]{2,1,0:T(8,128)(2,1)S(1)}, u32[]{:S(2)}, u32[]{:S(2)}) %all-to-all-start.2) | async-done | bytes 2097184 | tf_op jit(solution)/shard_map/all_to_all | solution.py:261
  128.3 4.6 %all-to-all-start.1 = ((bf16[32,192,128]{2,1,0:T(8,128)(2,1)}), bf16[32,192,128]{2,1,0:T(8,128)(2,1)S(1)}, u32[]{:S(2)}, u32[]{:S(2)}) async-start(bf16[32,192,128]{2,1,0:T(8,128)(2,1)} %get-tuple-element.23), calls=%async_computation.1 | async-start | bytes 3145728 | tf_op jit(solution)/shard_map/all_to_all | solution.py:261
  132.9 13.9 %attention1.1 = (bf16[32,192,128]{2,1,0:T(8,128)(2,1)}, bf16[4,64,128]{2,1,0:T(8,128)(2,1)}, bf16[4,64,128]{2,1,0:T(8,128)(2,1)}, bf16[4,64,128]{2,1,0:T(8,128)(...) custom-call(s32[1]{0:T(128)} %bitcast.group_ref, ...), custom_call_target="tpu_custom_call" | custom-call | flops 3221225472 | bytes 4194304 | tf_op jit(solution)/shard_map/attention1/pallas_call | solution.py:136
  146.8 25.4 %all-to-all-done.1.first_ref = bf16[32,192,128]{2,1,0:T(8,128)(2,1)S(1)} async-done(((bf16[32,192,128]{2,1,0:T(8,128)(2,1)}), bf16[32,192,128]{2,1,0:T(8,128)(2,1)S(1)}, u32[]{:S(2)}, u32[]{:S(2)}) %all-to-all-start.1) | async-done | bytes 1572896 | tf_op jit(solution)/shard_map/all_to_all | solution.py:261
  172.2 4.4 %all-to-all-start.3 = ((bf16[32,192,128]{2,1,0:T(8,128)(2,1)}), bf16[32,192,128]{2,1,0:T(8,128)(2,1)S(1)}, u32[]{:S(2)}, u32[]{:S(2)}) async-start(bf16[32,192,128]{2,1,0:T(8,128)(2,1)} %get-tuple-element.24), calls=%async_computation.3 | async-start | bytes 3145728 | tf_op jit(solution)/shard_map/all_to_all | solution.py:261
  176.6 7.2 %collective-permute-start = (bf16[4,64,128]{2,1,0:T(8,128)(2,1)S(1)}, bf16[4,64,128]{2,1,0:T(8,128)(2,1)S(1)}, u32[]{:S(2)}, u32[]{:S(2)}) collective-permute-start(bf16[4,64,128]{2,1,0:T(8,128)(2,1)S(1)} %copy-done.11), channel_id=1, source_target_pairs={{0,0},{1,1},{2,2},{3,3},{4,32},{5,33},{6,34},{7,35},{8,64},{9,65},... | collective-permute-start | bytes 196616 | tf_op jit(solution)/shard_map/ppermute | solution.py:293
  186.8 6.0 %collective-permute-start.4 = (bf16[4,64,128]{2,1,0:T(8,128)(2,1)}, bf16[4,64,128]{2,1,0:T(8,128)(2,1)S(1)}, u32[]{:S(2)}, u32[]{:S(2)}) collective-permute-start(bf16[4,64,128]{2,1,0:T(8,128)(2,1)} %get-tuple-element.29), channel_id=1, source_target_pairs={{0,16},{1,17},{2,18},{3,19},{4,48},{5,49},{6,50},{7,51},{8,80},{9,... | collective-permute-start | bytes 196616 | tf_op jit(solution)/shard_map/ppermute | solution.py:293
  192.8 25.8 %collective-permute-done.rest_0_ = bf16[4,64,128]{2,1,0:T(8,128)(2,1)S(1)} collective-permute-done((bf16[4,64,128]{2,1,0:T(8,128)(2,1)S(1)}, bf16[4,64,128]{2,1,0:T(8,128)(2,1)S(1)}, u32[]{:S(2)}, u32[]{:S(2)}) %collective-permute-start) | collective-permute-done | bytes 65568 | tf_op jit(solution)/shard_map/ppermute | solution.py:293
  218.6 3.5 %collective-permute-start.5 = (bf16[4,64,128]{2,1,0:T(8,128)(2,1)}, bf16[4,64,128]{2,1,0:T(8,128)(2,1)S(1)}, u32[]{:S(2)}, u32[]{:S(2)}) collective-permute-start(bf16[4,64,128]{2,1,0:T(8,128)(2,1)} %get-tuple-element.30), channel_id=1, source_target_pairs={{0,20},{1,21},{2,22},{3,23},{4,52},{5,53},{6,54},{7,55},{8,84},{9,... | collective-permute-start | bytes 196616 | tf_op jit(solution)/shard_map/ppermute | solution.py:293
  222.2 6.4 %collective-permute-start.6 = (bf16[4,64,128]{2,1,0:T(8,128)(2,1)}, bf16[4,64,128]{2,1,0:T(8,128)(2,1)}, u32[]{:S(2)}, u32[]{:S(2)}) collective-permute-start(bf16[4,64,128]{2,1,0:T(8,128)(2,1)} %get-tuple-element.31), channel_id=1, source_target_pairs={{0,24},{1,25},{2,26},{3,27},{4,56},{5,57},{6,58},{7,59},{8,88},{9,... | collective-permute-start | bytes 196616 | tf_op jit(solution)/shard_map/ppermute | solution.py:293
  228.6 6.1 %collective-permute-start.7 = (bf16[4,64,128]{2,1,0:T(8,128)(2,1)}, bf16[4,64,128]{2,1,0:T(8,128)(2,1)}, u32[]{:S(2)}, u32[]{:S(2)}) collective-permute-start(bf16[4,64,128]{2,1,0:T(8,128)(2,1)} %get-tuple-element.32), channel_id=1, source_target_pairs={{0,28},{1,29},{2,30},{3,31},{4,60},{5,61},{6,62},{7,63},{8,92},{9,... | collective-permute-start | bytes 196616 | tf_op jit(solution)/shard_map/ppermute | solution.py:293
  234.7 5.9 %collective-permute-start.8 = (bf16[4,64,128]{2,1,0:T(8,128)(2,1)}, bf16[4,64,128]{2,1,0:T(8,128)(2,1)}, u32[]{:S(2)}, u32[]{:S(2)}) collective-permute-start(bf16[4,64,128]{2,1,0:T(8,128)(2,1)} %get-tuple-element.33), channel_id=1, source_target_pairs={{0,0},{1,1},{2,2},{3,3},{4,32},{5,33},{6,34},{7,35},{8,64},{9,65},... | collective-permute-start | bytes 196616 | tf_op jit(solution)/shard_map/ppermute | solution.py:293
  240.9 5.3 %collective-permute-start.12 = (bf16[4,64,128]{2,1,0:T(8,128)(2,1)}, bf16[4,64,128]{2,1,0:T(8,128)(2,1)}, u32[]{:S(2)}, u32[]{:S(2)}) collective-permute-start(bf16[4,64,128]{2,1,0:T(8,128)(2,1)} %get-tuple-element.37), channel_id=1, source_target_pairs={{0,16},{1,17},{2,18},{3,19},{4,48},{5,49},{6,50},{7,51},{8,80},{9,... | collective-permute-start | bytes 196616 | tf_op jit(solution)/shard_map/ppermute | solution.py:293
  246.2 3.0 collective-permute-done.8.rest_8_
  250.3 4.6 %collective-permute-start.14 = (bf16[4,64,128]{2,1,0:T(8,128)(2,1)}, bf16[4,64,128]{2,1,0:T(8,128)(2,1)}, u32[]{:S(2)}, u32[]{:S(2)}) collective-permute-start(bf16[4,64,128]{2,1,0:T(8,128)(2,1)} %get-tuple-element.39), channel_id=1, source_target_pairs={{0,24},{1,25},{2,26},{3,27},{4,56},{5,57},{6,58},{7,59},{8,88},{9,... | collective-permute-start | bytes 196616 | tf_op jit(solution)/shard_map/ppermute | solution.py:293
  255.0 4.4 %collective-permute-start.15 = (bf16[4,64,128]{2,1,0:T(8,128)(2,1)}, bf16[4,64,128]{2,1,0:T(8,128)(2,1)}, u32[]{:S(2)}, u32[]{:S(2)}) collective-permute-start(bf16[4,64,128]{2,1,0:T(8,128)(2,1)} %get-tuple-element.40), channel_id=1, source_target_pairs={{0,28},{1,29},{2,30},{3,31},{4,60},{5,61},{6,62},{7,63},{8,92},{9,... | collective-permute-start | bytes 196616 | tf_op jit(solution)/shard_map/ppermute | solution.py:293
  265.0 15.4 %tiles.1 = bf16[32,128,128]{2,1,0:T(8,128)(2,1)} custom-call(s32[2]{0:T(128)} %pad_add_fusion.where_ref, bf16[32,128,4096]{2,1,0:T(8,128)(2,1)} %bitcast.8, bf16[4,64,128]{2,1,0:T(8,128)(2,1)} %copy-done.4, bf16[4,64,128]{2,1,0:T(8,128)(2,1)} %copy-done.5, bf16[4,64,128]{2,1,0:T(8,128)(2,1)} %copy-done.6, bf16[4,64,128]{2,1,0:T(8,128)(2,1)} %copy-done.7, ...), custom_call_target="tpu_custom_call" | custom-call | flops 4294967296 | bytes 35651584 | tf_op jit(solution)/shard_map/tiles/pallas_call | solution.py:209
  280.4 38.4 %reduce-scatter.2.cloned.1.call-done = bf16[1,512,128]{2,1,0:T(8,128)(2,1)} async-done(((bf16[8,512,128]{2,1,0:T(8,128)(2,1)}), bf16[1,512,128]{2,1,0:T(8,128)(2,1)}) %reduce-scatter.2.cloned.1.call-update) | async-done | bytes 131088 | tf_op jit(solution)/shard_map/reduce_scatter | solution.py:298
  318.9 5.0 %collective-permute-start.16 = (bf16[512,128]{1,0:T(8,128)(2,1)}, bf16[512,128]{1,0:T(8,128)(2,1)S(1)}, u32[]{:S(2)}, u32[]{:S(2)}) collective-permute-start(bf16[512,128]{1,0:T(8,128)(2,1)} %bitcast.11), channel_id=1, source_target_pairs={{0,0},{1,1},{2,2},{3,3},{4,36},{5,37},{6,38},{7,39},{8,72},{9,73},... | collective-permute-start | bytes 393224 | tf_op jit(solution)/shard_map/ppermute | solution.py:301
  325.0 3.5 %unpack.1 = bf16[3,2,64,4096]{3,2,1,0:T(8,128)(2,1)} custom-call(bf16[32,192,128]{2,1,0:T(8,128)(2,1)} %copy-done, bf16[32,192,128]{2,1,0:T(8,128)(2,1)} %copy-done.1), custom_call_target="tpu_custom_call" | custom-call | bytes 6291456 | tf_op jit(solution)/shard_map/unpack/pallas_call | solution.py:169
  (56 shorter events, 24.5 us)
Async XLA Ops:
  7.2 257.8 %all-gather.2.cloned.1.call-start = ((), (), s32[]{:S(2)}) async-start(), calls=%async_computation.5 | async-start | bytes 34603008 | tf_op jit(solution)/shard_map/all_gather | solution.py:286
  10.6 60.2 %all-to-all-start = ((bf16[32,256,128]{2,1,0:T(8,128)(2,1)}), bf16[32,256,128]{2,1,0:T(8,128)(2,1)S(1)}, u32[]{:S(2)}, u32[]{:S(2)}) async-start(bf16[32,256,128]{2,1,0:T(8,128)(2,1)} %pack0.1), calls=%async_computation | async-start | bytes 4194304 | tf_op jit(solution)/shard_map/all_to_all | solution.py:261
  72.1 54.9 %all-to-all-start.2 = ((bf16[32,256,128]{2,1,0:T(8,128)(2,1)}), bf16[32,256,128]{2,1,0:T(8,128)(2,1)S(1)}, u32[]{:S(2)}, u32[]{:S(2)}) async-start(bf16[32,256,128]{2,1,0:T(8,128)(2,1)} %pack1.1), calls=%async_computation.2 | async-start | bytes 4194304 | tf_op jit(solution)/shard_map/all_to_all | solution.py:261
  128.3 43.9 %all-to-all-start.1 = ((bf16[32,192,128]{2,1,0:T(8,128)(2,1)}), bf16[32,192,128]{2,1,0:T(8,128)(2,1)S(1)}, u32[]{:S(2)}, u32[]{:S(2)}) async-start(bf16[32,192,128]{2,1,0:T(8,128)(2,1)} %get-tuple-element.23), calls=%async_computation.1 | async-start | bytes 3145728 | tf_op jit(solution)/shard_map/all_to_all | solution.py:261
  172.2 108.2 %copy-start = (bf16[32,192,128]{2,1,0:T(8,128)(2,1)}, bf16[32,192,128]{2,1,0:T(8,128)(2,1)S(1)}, u32[]{:S(2)}) copy-start(bf16[32,192,128]{2,1,0:T(8,128)(2,1)S(1)} %all-to-all-done.1.first_ref) | copy-start | bytes 4718596
  172.2 151.6 %all-to-all-start.3 = ((bf16[32,192,128]{2,1,0:T(8,128)(2,1)}), bf16[32,192,128]{2,1,0:T(8,128)(2,1)S(1)}, u32[]{:S(2)}, u32[]{:S(2)}) async-start(bf16[32,192,128]{2,1,0:T(8,128)(2,1)} %get-tuple-element.24), calls=%async_computation.3 | async-start | bytes 3145728 | tf_op jit(solution)/shard_map/all_to_all | solution.py:261
  176.6 142.3 %reduce-scatter.2.cloned.1.call-start = ((), (), s32[]{:S(2)}) async-start(), calls=%async_computation.6 | async-start | bytes 1179648 | tf_op jit(solution)/shard_map/reduce_scatter | solution.py:298
  176.6 42.0 %collective-permute-start = (bf16[4,64,128]{2,1,0:T(8,128)(2,1)S(1)}, bf16[4,64,128]{2,1,0:T(8,128)(2,1)S(1)}, u32[]{:S(2)}, u32[]{:S(2)}) collective-permute-start(bf16[4,64,128]{2,1,0:T(8,128)(2,1)S(1)} %copy-done.11), channel_id=1, source_target_pairs={{0,0},{1,1},{2,2},{3,3},{4,32},{5,33},{6,34},{7,35},{8,64},{9,65},... | collective-permute-start | bytes 196616 | tf_op jit(solution)/shard_map/ppermute | solution.py:293
  183.8 38.3 %collective-permute-start.1 = (bf16[4,64,128]{2,1,0:T(8,128)(2,1)}, bf16[4,64,128]{2,1,0:T(8,128)(2,1)S(1)}, u32[]{:S(2)}, u32[]{:S(2)}) collective-permute-start(bf16[4,64,128]{2,1,0:T(8,128)(2,1)} %get-tuple-element.26), channel_id=1, source_target_pairs={{0,4},{1,5},{2,6},{3,7},{4,36},{5,37},{6,38},{7,39},{8,68},{9,69},... | collective-permute-start | bytes 196616 | tf_op jit(solution)/shard_map/ppermute | solution.py:293
  186.6 41.9 %collective-permute-start.2 = (bf16[4,64,128]{2,1,0:T(8,128)(2,1)}, bf16[4,64,128]{2,1,0:T(8,128)(2,1)S(1)}, u32[]{:S(2)}, u32[]{:S(2)}) collective-permute-start(bf16[4,64,128]{2,1,0:T(8,128)(2,1)} %get-tuple-element.27), channel_id=1, source_target_pairs={{0,8},{1,9},{2,10},{3,11},{4,40},{5,41},{6,42},{7,43},{8,72},{9,73... | collective-permute-start | bytes 196616 | tf_op jit(solution)/shard_map/ppermute | solution.py:293
  186.6 48.0 %collective-permute-start.3 = (bf16[4,64,128]{2,1,0:T(8,128)(2,1)}, bf16[4,64,128]{2,1,0:T(8,128)(2,1)S(1)}, u32[]{:S(2)}, u32[]{:S(2)}) collective-permute-start(bf16[4,64,128]{2,1,0:T(8,128)(2,1)} %get-tuple-element.28), channel_id=1, source_target_pairs={{0,12},{1,13},{2,14},{3,15},{4,44},{5,45},{6,46},{7,47},{8,76},{9,... | collective-permute-start | bytes 196616 | tf_op jit(solution)/shard_map/ppermute | solution.py:293
  186.8 53.7 %collective-permute-start.4 = (bf16[4,64,128]{2,1,0:T(8,128)(2,1)}, bf16[4,64,128]{2,1,0:T(8,128)(2,1)S(1)}, u32[]{:S(2)}, u32[]{:S(2)}) collective-permute-start(bf16[4,64,128]{2,1,0:T(8,128)(2,1)} %get-tuple-element.29), channel_id=1, source_target_pairs={{0,16},{1,17},{2,18},{3,19},{4,48},{5,49},{6,50},{7,51},{8,80},{9,... | collective-permute-start | bytes 196616 | tf_op jit(solution)/shard_map/ppermute | solution.py:293
  218.6 22.0 %collective-permute-start.5 = (bf16[4,64,128]{2,1,0:T(8,128)(2,1)}, bf16[4,64,128]{2,1,0:T(8,128)(2,1)S(1)}, u32[]{:S(2)}, u32[]{:S(2)}) collective-permute-start(bf16[4,64,128]{2,1,0:T(8,128)(2,1)} %get-tuple-element.30), channel_id=1, source_target_pairs={{0,20},{1,21},{2,22},{3,23},{4,52},{5,53},{6,54},{7,55},{8,84},{9,... | collective-permute-start | bytes 196616 | tf_op jit(solution)/shard_map/ppermute | solution.py:293
  222.2 18.6 %collective-permute-start.6 = (bf16[4,64,128]{2,1,0:T(8,128)(2,1)}, bf16[4,64,128]{2,1,0:T(8,128)(2,1)}, u32[]{:S(2)}, u32[]{:S(2)}) collective-permute-start(bf16[4,64,128]{2,1,0:T(8,128)(2,1)} %get-tuple-element.31), channel_id=1, source_target_pairs={{0,24},{1,25},{2,26},{3,27},{4,56},{5,57},{6,58},{7,59},{8,88},{9,... | collective-permute-start | bytes 196616 | tf_op jit(solution)/shard_map/ppermute | solution.py:293
  228.6 12.3 %collective-permute-start.7 = (bf16[4,64,128]{2,1,0:T(8,128)(2,1)}, bf16[4,64,128]{2,1,0:T(8,128)(2,1)}, u32[]{:S(2)}, u32[]{:S(2)}) collective-permute-start(bf16[4,64,128]{2,1,0:T(8,128)(2,1)} %get-tuple-element.32), channel_id=1, source_target_pairs={{0,28},{1,29},{2,30},{3,31},{4,60},{5,61},{6,62},{7,63},{8,92},{9,... | collective-permute-start | bytes 196616 | tf_op jit(solution)/shard_map/ppermute | solution.py:293
  234.7 14.5 %collective-permute-start.8 = (bf16[4,64,128]{2,1,0:T(8,128)(2,1)}, bf16[4,64,128]{2,1,0:T(8,128)(2,1)}, u32[]{:S(2)}, u32[]{:S(2)}) collective-permute-start(bf16[4,64,128]{2,1,0:T(8,128)(2,1)} %get-tuple-element.33), channel_id=1, source_target_pairs={{0,0},{1,1},{2,2},{3,3},{4,32},{5,33},{6,34},{7,35},{8,64},{9,65},... | collective-permute-start | bytes 196616 | tf_op jit(solution)/shard_map/ppermute | solution.py:293
  240.6 9.8 %collective-permute-start.9 = (bf16[4,64,128]{2,1,0:T(8,128)(2,1)}, bf16[4,64,128]{2,1,0:T(8,128)(2,1)}, u32[]{:S(2)}, u32[]{:S(2)}) collective-permute-start(bf16[4,64,128]{2,1,0:T(8,128)(2,1)} %get-tuple-element.34), channel_id=1, source_target_pairs={{0,4},{1,5},{2,6},{3,7},{4,36},{5,37},{6,38},{7,39},{8,68},{9,69},... | collective-permute-start | bytes 196616 | tf_op jit(solution)/shard_map/ppermute | solution.py:293
  240.7 14.3 %collective-permute-start.10 = (bf16[4,64,128]{2,1,0:T(8,128)(2,1)}, bf16[4,64,128]{2,1,0:T(8,128)(2,1)}, u32[]{:S(2)}, u32[]{:S(2)}) collective-permute-start(bf16[4,64,128]{2,1,0:T(8,128)(2,1)} %get-tuple-element.35), channel_id=1, source_target_pairs={{0,8},{1,9},{2,10},{3,11},{4,40},{5,41},{6,42},{7,43},{8,72},{9,73... | collective-permute-start | bytes 196616 | tf_op jit(solution)/shard_map/ppermute | solution.py:293
  240.8 19.2 %collective-permute-start.11 = (bf16[4,64,128]{2,1,0:T(8,128)(2,1)}, bf16[4,64,128]{2,1,0:T(8,128)(2,1)}, u32[]{:S(2)}, u32[]{:S(2)}) collective-permute-start(bf16[4,64,128]{2,1,0:T(8,128)(2,1)} %get-tuple-element.36), channel_id=1, source_target_pairs={{0,12},{1,13},{2,14},{3,15},{4,44},{5,45},{6,46},{7,47},{8,76},{9,... | collective-permute-start | bytes 196616 | tf_op jit(solution)/shard_map/ppermute | solution.py:293
  240.9 19.1 %collective-permute-start.12 = (bf16[4,64,128]{2,1,0:T(8,128)(2,1)}, bf16[4,64,128]{2,1,0:T(8,128)(2,1)}, u32[]{:S(2)}, u32[]{:S(2)}) collective-permute-start(bf16[4,64,128]{2,1,0:T(8,128)(2,1)} %get-tuple-element.37), channel_id=1, source_target_pairs={{0,16},{1,17},{2,18},{3,19},{4,48},{5,49},{6,50},{7,51},{8,80},{9,... | collective-permute-start | bytes 196616 | tf_op jit(solution)/shard_map/ppermute | solution.py:293
  249.2 10.7 %collective-permute-start.13 = (bf16[4,64,128]{2,1,0:T(8,128)(2,1)}, bf16[4,64,128]{2,1,0:T(8,128)(2,1)}, u32[]{:S(2)}, u32[]{:S(2)}) collective-permute-start(bf16[4,64,128]{2,1,0:T(8,128)(2,1)} %get-tuple-element.38), channel_id=1, source_target_pairs={{0,20},{1,21},{2,22},{3,23},{4,52},{5,53},{6,54},{7,55},{8,84},{9,... | collective-permute-start | bytes 196616 | tf_op jit(solution)/shard_map/ppermute | solution.py:293
  250.3 12.5 %collective-permute-start.14 = (bf16[4,64,128]{2,1,0:T(8,128)(2,1)}, bf16[4,64,128]{2,1,0:T(8,128)(2,1)}, u32[]{:S(2)}, u32[]{:S(2)}) collective-permute-start(bf16[4,64,128]{2,1,0:T(8,128)(2,1)} %get-tuple-element.39), channel_id=1, source_target_pairs={{0,24},{1,25},{2,26},{3,27},{4,56},{5,57},{6,58},{7,59},{8,88},{9,... | collective-permute-start | bytes 196616 | tf_op jit(solution)/shard_map/ppermute | solution.py:293
  255.0 10.0 %collective-permute-start.15 = (bf16[4,64,128]{2,1,0:T(8,128)(2,1)}, bf16[4,64,128]{2,1,0:T(8,128)(2,1)}, u32[]{:S(2)}, u32[]{:S(2)}) collective-permute-start(bf16[4,64,128]{2,1,0:T(8,128)(2,1)} %get-tuple-element.40), channel_id=1, source_target_pairs={{0,28},{1,29},{2,30},{3,31},{4,60},{5,61},{6,62},{7,63},{8,92},{9,... | collective-permute-start | bytes 196616 | tf_op jit(solution)/shard_map/ppermute | solution.py:293
  318.9 11.0 %collective-permute-start.16 = (bf16[512,128]{1,0:T(8,128)(2,1)}, bf16[512,128]{1,0:T(8,128)(2,1)S(1)}, u32[]{:S(2)}, u32[]{:S(2)}) collective-permute-start(bf16[512,128]{1,0:T(8,128)(2,1)} %bitcast.11), channel_id=1, source_target_pairs={{0,0},{1,1},{2,2},{3,3},{4,36},{5,37},{6,38},{7,39},{8,72},{9,73},... | collective-permute-start | bytes 393224 | tf_op jit(solution)/shard_map/ppermute | solution.py:301
  (11 other events, 239.0 us)
Sparse Core Ops, SparseCore 0:
  10.6 180.9 all-gather.1
  280.5 38.2 reduce-scatter.1

commit v3 on v1

--- a/solution.py
+++ b/solution.py
@@ -22,6 +22,7 @@
 LEN = N_CTX * TOK
 BLOCK = 256
 PAD = 8
+VMEM = 60 << 20
 
 
 def nt_dot(a, b):
@@ -41,7 +42,7 @@
         out_ref[c, 3 * TOK : 4 * TOK, :] = dout_ref[0, :, lanes]
 
 
-def pack(qkv_pre, d_out, seq, width=8):
+def pack(qkv_pre, d_out, seq, width=16):
     return pl.pallas_call(
         pack_kernel,
         grid=(N_CTX // width,),
@@ -51,6 +52,7 @@
         ],
         out_specs=pl.BlockSpec((width, 4 * TOK, HDIM), lambda i: (i, 0, 0)),
         out_shape=jax.ShapeDtypeStruct((N_CTX, 4 * TOK, HDIM), jnp.bfloat16),
+        compiler_params=pltpu.CompilerParams(vmem_limit_bytes=VMEM),
         name=f"pack{seq}",
         cost_estimate=pl.CostEstimate(flops=0, bytes_accessed=4 << 20, transcendentals=0),
     )(qkv_pre, d_out)
@@ -147,7 +149,7 @@
             pltpu.VMEM((LEN, BLOCK), jnp.float32),
             pltpu.VMEM((3, LEN + PAD, HDIM), jnp.float32),
         ],
-        compiler_params=pltpu.CompilerParams(vmem_limit_bytes=32 << 20),
+        compiler_params=pltpu.CompilerParams(vmem_limit_bytes=VMEM),
         name=f"attention{seq}",
         cost_estimate=pl.CostEstimate(
             flops=6 * LEN * LEN * HDIM, bytes_accessed=4 << 20, transcendentals=LEN * LEN // 2
@@ -155,52 +157,43 @@
     )(received, taps)
 
 
-def unpack_kernel(q0_ref, kv0_ref, q1_ref, kv1_ref, out_ref):
+def unpack_kernel(q0_ref, q1_ref, kv_ref, out_ref):
     for c in range(q0_ref.shape[0]):
         lanes = slice(c * HDIM, (c + 1) * HDIM)
-        for seq, (q_ref, kv_ref) in enumerate(((q0_ref, kv0_ref), (q1_ref, kv1_ref))):
+        for seq, q_ref in enumerate((q0_ref, q1_ref)):
+            first = 2 * seq * TOK
             out_ref[0, seq, :, lanes] = q_ref[c]
-            out_ref[1, seq, :, lanes] = kv_ref[c, 0:TOK, :]
-            out_ref[2, seq, :, lanes] = kv_ref[c, TOK : 2 * TOK, :]
-
-
-def unpack(q0, kv0, q1, kv1, width=8):
+            out_ref[1, seq, :, lanes] = kv_ref[c, first : first + TOK, :]
+            out_ref[2, seq, :, lanes] = kv_ref[c, first + TOK : first + 2 * TOK, :]
+
+
+def unpack(q0, q1, kv, width=16):
     q_spec = pl.BlockSpec((width, TOK, HDIM), lambda i: (i, 0, 0))
-    kv_spec = pl.BlockSpec((width, 2 * TOK, HDIM), lambda i: (i, 0, 0))
+    kv_spec = pl.BlockSpec((width, 4 * TOK, HDIM), lambda i: (i, 0, 0))
     return pl.pallas_call(
         unpack_kernel,
         grid=(N_CTX // width,),
-        in_specs=[q_spec, kv_spec, q_spec, kv_spec],
+        in_specs=[q_spec, q_spec, kv_spec],
         out_specs=pl.BlockSpec((3, 2, TOK, width * HDIM), lambda i: (0, 0, 0, i)),
         out_shape=jax.ShapeDtypeStruct((3, 2, TOK, N_CTX * HDIM), jnp.bfloat16),
+        compiler_params=pltpu.CompilerParams(vmem_limit_bytes=VMEM),
         name="unpack",
         cost_estimate=pl.CostEstimate(flops=0, bytes_accessed=6 << 20, transcendentals=0),
-    )(q0, kv0, q1, kv1)
-
-
-FEATS = 512
-
-
-def tiles_first_kernel(grad_ref, x_ref, out_ref, gt_ref):
-    @pl.when(pl.program_id(0) == 0)
-    def _():
-        full = grad_ref[...].reshape(LEN, HDIM).astype(jnp.float32)
-        gt_ref[...] = jnp.transpose(full).astype(jnp.bfloat16)
-
-    out_ref[...] = nn_dot(gt_ref[...], x_ref[:, 0].reshape(LEN, FEATS))
-
-
-def tiles_second_kernel(lane_ref, grad_ref, x_ref, first_ref, out_ref, gt_ref):
+    )(q0, q1, kv)
+
+
+FEATS = 1024
+
+
+def tiles_kernel(lane_ref, grad_ref, x_ref, out_ref, gt_ref):
     step = pl.program_id(0)
 
     @pl.when(step == 0)
     def _():
-        full = grad_ref[...].reshape(LEN, HDIM).astype(jnp.float32)
+        full = grad_ref[...].reshape(2 * LEN, HDIM).astype(jnp.float32)
         gt_ref[...] = jnp.transpose(full).astype(jnp.bfloat16)
 
-    done = (first_ref[...] + nn_dot(gt_ref[...], x_ref[:, 0].reshape(LEN, FEATS))).astype(
-        jnp.bfloat16
-    )
+    done = nn_dot(gt_ref[...], x_ref[...].reshape(2 * LEN, FEATS)).astype(jnp.bfloat16)
     for k in range(FEATS // HDIM):
         ahead = (step * (FEATS // HDIM) + k - lane_ref[0] + N_CTX) & (N_CTX - 1)
         offset = (SPAN - (ahead & (SPAN - 1))) & (SPAN - 1)
@@ -208,46 +201,29 @@
         out_ref[plane * SPAN + offset] = done[:, k * HDIM : (k + 1) * HDIM]
 
 
-def tile_sums(grad0, grad1, gathered, lane):
-    steps = N_CTX * HDIM // FEATS
-    cost = pl.CostEstimate(
-        flops=2 * LEN * HDIM * HDIM * N_CTX, bytes_accessed=20 << 20, transcendentals=0
-    )
-    grad_spec = pl.BlockSpec((N_CTX, TOK, HDIM), lambda i: (0, 0, 0))
-    acc_spec = pl.BlockSpec((HDIM, FEATS), lambda i: (0, i))
-    params = pltpu.CompilerParams(vmem_limit_bytes=24 << 20)
-    first = pl.pallas_call(
-        tiles_first_kernel,
-        grid=(steps,),
-        in_specs=[grad_spec, pl.BlockSpec((N_CTX, 1, TOK, FEATS), lambda i: (0, 0, 0, i))],
-        out_specs=acc_spec,
-        out_shape=jax.ShapeDtypeStruct((HDIM, N_CTX * HDIM), jnp.float32),
-        scratch_shapes=[pltpu.VMEM((HDIM, LEN), jnp.bfloat16)],
-        compiler_params=params,
-        name="tiles0",
-        cost_estimate=cost,
-    )(grad0, gathered)
-    return pl.pallas_call(
-        tiles_second_kernel,
-        grid=(steps,),
+def tile_sums(grads, gathered, lane):
+    return pl.pallas_call(
+        tiles_kernel,
+        grid=(N_CTX * HDIM // FEATS,),
         in_specs=[
             pl.BlockSpec(memory_space=pltpu.SMEM),
-            grad_spec,
-            pl.BlockSpec((N_CTX, 1, TOK, FEATS), lambda i: (0, 1, 0, i)),
-            acc_spec,
+            pl.BlockSpec((N_CTX, 2 * TOK, HDIM), lambda i: (0, 0, 0)),
+            pl.BlockSpec((N_CTX, 2 * TOK, FEATS), lambda i: (0, 0, i)),
         ],
         out_specs=pl.BlockSpec((N_CTX, HDIM, HDIM), lambda i: (0, 0, 0)),
         out_shape=jax.ShapeDtypeStruct((N_CTX, HDIM, HDIM), jnp.bfloat16),
-        scratch_shapes=[pltpu.VMEM((HDIM, LEN), jnp.bfloat16)],
-        compiler_params=params,
-        name="tiles1",
-        cost_estimate=cost,
-    )(lane, grad1, gathered, first)
+        scratch_shapes=[pltpu.VMEM((HDIM, 2 * LEN), jnp.bfloat16)],
+        compiler_params=pltpu.CompilerParams(vmem_limit_bytes=VMEM),
+        name="tiles",
+        cost_estimate=pl.CostEstimate(
+            flops=4 * LEN * HDIM * HDIM * N_CTX, bytes_accessed=34 << 20, transcendentals=0
+        ),
+    )(lane, grads, gathered)
 
 
 def gram_kernel(tile_ref, left_ref, right_ref, new_left_ref, new_right_ref):
     for s in range(SPAN):
-        tile_t = tile_ref[s] * (1.0 / math.sqrt(2 * N_DP * LEN))
+        tile_t = tile_ref[s].astype(jnp.float32) * (1.0 / math.sqrt(2 * N_DP * LEN))
         tile = jnp.transpose(tile_t)
         left = lax.dot(
             tile, tile_t, precision=lax.Precision.HIGHEST, preferred_element_type=jnp.float32
@@ -267,6 +243,7 @@
         in_specs=[vmem] * 3,
         out_specs=[vmem] * 2,
         out_shape=[shape, shape],
+        compiler_params=pltpu.CompilerParams(vmem_limit_bytes=VMEM),
         name="grams",
         cost_estimate=pl.CostEstimate(
             flops=6 * 16 * HDIM**3, bytes_accessed=1 << 20, transcendentals=0
@@ -288,19 +265,20 @@
 
 def on_device(qkv_pre, d_out, inputs, conv_taps, left_old, right_old):
     gathered = lax.all_gather(inputs.reshape(2 * TOK, N_CTX * HDIM), PLANE, axis=0, tiled=True)
-    gathered = gathered.reshape(N_CTX, 2, TOK, N_CTX * HDIM)
+    gathered = gathered.reshape(N_CTX, 2 * TOK, N_CTX * HDIM)
 
     received = [swap(pack(qkv_pre, d_out, seq), CTX) for seq in range(2)]
     gq, gkv = zip(*[attention(received[seq], conv_taps, seq) for seq in range(2)])
     gq = [swap(part, CTX) for part in gq]
-    gkv = [swap(part, CTX) for part in gkv]
-    grad_qkv = unpack(gq[0], gkv[0], gq[1], gkv[1])
-
-    columns = [swap(part, PLANE) for part in gq]
+    columns = swap(jnp.concatenate(gq, axis=1), PLANE)
+    gkv = swap(jnp.concatenate(gkv, axis=1), CTX)
+    grad_qkv = unpack(gq[0], gq[1], gkv)
+
     lane = (lax.axis_index("yl") * 2 + lax.axis_index("core")).astype(jnp.int32).reshape(1)
-    partial = tile_sums(columns[0], columns[1], gathered, lane)
-    arrived = swap(partial.reshape(N_Z, SPAN * HDIM, HDIM), "z")
-    summed = jnp.sum(arrived.astype(jnp.float32), axis=0)
+    partial = tile_sums(columns, gathered, lane)
+    summed = lax.psum_scatter(
+        partial.reshape(N_Z, SPAN * HDIM, HDIM), "z", scatter_dimension=0, tiled=True
+    )[0]
     tiles = lax.ppermute(summed, ALL, owner_pairs()).reshape(SPAN, HDIM, HDIM)
     new_left, new_right = grams(tiles, left_old, right_old)
     return (grad_qkv, new_left, new_right)

time: 320 us -> 284 us (0.89); the launches traced: 316 us -> 284 us
  blocking collectives: 83.2 us -> 21.9 us
  waiting for transfers between devices: 121 us -> 150 us
  Pallas kernels: 57.7 us -> 52.2 us
  other arithmetic: 0.15 us -> 3.79 us
    all_to_all x4 -> x1, blocking collectives: 83.2 us -> 21.9 us  [swap(): return lax.all_to_all(value, axes, split_axis=0, concat_axis=0, tiled=True)]
    reduce_scatter x0 -> x1, waiting for transfers between devices: none -> 48.6 us  [on_device(): lax.psum_scatter(partial.reshape(N_Z, SPAN * HDIM, HDIM), 'z', scatter_di...]
    all_to_all x5, waiting for transfers between devices: 121 us -> 99 us  [swap(): return lax.all_to_all(value, axes, split_axis=0, concat_axis=0, tiled=True)]
    pallas_call x3 -> x2, Pallas kernels: 23.9 us -> 17.1 us  [the longest x1 13.6 us: tile_sums(): pl.pallas_call(tiles_kernel, grid=(N_CTX * HDIM // FEATS,), in_specs=[pl....]
    concatenate x0 -> x2, other arithmetic: none -> 3.79 us  [the longest x1 2.73 us: on_device(): gkv = swap(jnp.concatenate(gkv, axis=1), CTX)]
    pallas_call x2, Pallas kernels: 23.5 us -> 27.2 us  [attention(): pl.pallas_call(attention_kernel, in_specs=[vmem, vmem], out_specs=[vmem,...]
  transfers between devices with their start and end apart: 7 -> 8, of which waited for: 5 -> 6; matrix products, arithmetic and copies ran while one was open for 0% -> 1% of each run, Pallas kernels for 17% -> 18%
where the time goes in v3:
time: 284 us
  waiting for transfers between devices  150 us (53%)
  Pallas kernels  52.2 us (18%)
  starting transfers between devices  37.3 us (13%)
  blocking collectives  21.9 us (8%)
  between operations  14.1 us (5%)
  local copies, waits for them, and re-layouts  4.35 us (2%)
  other arithmetic  3.79 us (1%)
    all_to_all x5, waiting for transfers between devices, swap(): return lax.all_to_all(value, axes, split_axis=0, concat_axis=0, tiled=True)  99 us
    reduce_scatter x1, waiting for transfers between devices, on_device(): lax.psum_scatter(partial.reshape(N_Z, SPAN * HDIM, HDIM), 'z', scatter_di...  48.6 us
    all_to_all x5, starting transfers between devices, swap(): return lax.all_to_all(value, axes, split_axis=0, concat_axis=0, tiled=True)  32.6 us
    pallas_call x2, Pallas kernels, attention(): pl.pallas_call(attention_kernel, in_specs=[vmem, vmem], out_specs=[vmem,...  27.2 us
    all_to_all x1, blocking collectives, swap(): return lax.all_to_all(value, axes, split_axis=0, concat_axis=0, tiled=True)  21.9 us
    pallas_call x1, Pallas kernels, tile_sums(): pl.pallas_call(tiles_kernel, grid=(N_CTX * HDIM // FEATS,), in_specs=[pl....  13.6 us
  transfers between devices with their start and end apart: 8, of which 6 were waited for; matrix products, arithmetic and copies ran while one was open for 1% of the time, Pallas kernels for 18%

profile of v3, /device:TPU:46, one launch (start us, length us, event | category | flops | bytes accessed | tf_op | source)
XLA Modules:
  0.0 283.5 jit_solution(11816375267112583290)
XLA Ops:
  7.9 2.7 pack0.1
  10.6 9.6 %all-to-all-start = ((bf16[32,256,128]{2,1,0:T(8,128)(2,1)}), bf16[32,256,128]{2,1,0:T(8,128)(2,1)S(1)}, u32[]{:S(2)}, u32[]{:S(2)}) async-start(bf16[32,256,128]{2,1,0:T(8,128)(2,1)} %pack0.1), calls=%async_computation | async-start | bytes 4194304 | tf_op jit(solution)/shard_map/all_to_all | solution.py:255
  20.2 2.7 pack1.1
  22.9 47.8 %all-to-all-done.recv_ref = bf16[32,256,128]{2,1,0:T(8,128)(2,1)S(1)} async-done(((bf16[32,256,128]{2,1,0:T(8,128)(2,1)}), bf16[32,256,128]{2,1,0:T(8,128)(2,1)S(1)}, u32[]{:S(2)}, u32[]{:S(2)}) %all-to-all-start) | async-done | bytes 2097184 | tf_op jit(solution)/shard_map/all_to_all | solution.py:255
  70.8 1.3 copy-done.5
  72.1 4.4 %all-to-all-start.2 = ((bf16[32,256,128]{2,1,0:T(8,128)(2,1)}), bf16[32,256,128]{2,1,0:T(8,128)(2,1)S(1)}, u32[]{:S(2)}, u32[]{:S(2)}) async-start(bf16[32,256,128]{2,1,0:T(8,128)(2,1)} %pack1.1), calls=%async_computation.2 | async-start | bytes 4194304 | tf_op jit(solution)/shard_map/all_to_all | solution.py:255
  76.5 13.7 %attention0.1 = (bf16[32,64,128]{2,1,0:T(8,128)(2,1)}, bf16[32,128,128]{2,1,0:T(8,128)(2,1)}) custom-call(bf16[32,256,128]{2,1,0:T(8,128)(2,1)} %copy-done.5, f32[3,3,128]{2,1,0:T(4,128)} %taps_ref.3), custom_call_target="tpu_custom_call" | custom-call | flops 3221225472 | bytes 4194304 | tf_op jit(solution)/shard_map/attention0/pallas_call | solution.py:136
  90.2 36.8 %all-to-all-done.2.recv_ref = bf16[32,256,128]{2,1,0:T(8,128)(2,1)S(1)} async-done(((bf16[32,256,128]{2,1,0:T(8,128)(2,1)}), bf16[32,256,128]{2,1,0:T(8,128)(2,1)S(1)}, u32[]{:S(2)}, u32[]{:S(2)}) %all-to-all-start.2) | async-done | bytes 2097184 | tf_op jit(solution)/shard_map/all_to_all | solution.py:255
  127.0 4.4 %all-to-all-start.1 = ((bf16[32,64,128]{2,1,0:T(8,128)(2,1)}), bf16[32,64,128]{2,1,0:T(8,128)(2,1)S(1)}, u32[]{:S(2)}, u32[]{:S(2)}) async-start(bf16[32,64,128]{2,1,0:T(8,128)(2,1)} %get-tuple-element.9), calls=%async_computation.1 | async-start | bytes 1048576 | tf_op jit(solution)/shard_map/all_to_all | solution.py:255
  131.4 13.4 %attention1.1 = (bf16[32,64,128]{2,1,0:T(8,128)(2,1)}, bf16[32,128,128]{2,1,0:T(8,128)(2,1)}) custom-call(bf16[32,256,128]{2,1,0:T(8,128)(2,1)} %copy-done.4, f32[3,3,128]{2,1,0:T(4,128)} %taps_ref.3), custom_call_target="tpu_custom_call" | custom-call | flops 3221225472 | bytes 4194304 | tf_op jit(solution)/shard_map/attention1/pallas_call | solution.py:136
  144.9 3.4 %all-to-all-done.1.q0_ref = bf16[32,64,128]{2,1,0:T(8,128)(2,1)S(1)} async-done(((bf16[32,64,128]{2,1,0:T(8,128)(2,1)}), bf16[32,64,128]{2,1,0:T(8,128)(2,1)S(1)}, u32[]{:S(2)}, u32[]{:S(2)}) %all-to-all-start.1) | async-done | bytes 524320 | tf_op jit(solution)/shard_map/all_to_all | solution.py:255
  148.3 21.9 %all_to_all.30.q1_ref = bf16[32,64,128]{2,1,0:T(8,128)(2,1)S(1)} all-to-all(bf16[32,64,128]{2,1,0:T(8,128)(2,1)} %get-tuple-element.10), channel_id=1, replica_groups=mesh['x'=4,'yh'=2,'z'=8,'yl'=2,'core'=2] {'z','yl','core'}, dimensions={0} | all-to-all | bytes 1048576 | tf_op jit(solution)/shard_map/all_to_all | solution.py:255
  170.2 1.1 pad_maximum_fusion.1
  171.3 7.3 %all-to-all-start.5 = ((bf16[32,128,128]{2,1,0:T(8,128)(2,1)}), bf16[32,128,128]{2,1,0:T(8,128)(2,1)S(1)}, u32[]{:S(2)}, u32[]{:S(2)}) async-start(bf16[32,128,128]{2,1,0:T(8,128)(2,1)} %pad_maximum_fusion.1), calls=%async_computation.5 | async-start | bytes 2097152 | tf_op jit(solution)/shard_map/all_to_all | solution.py:255
  178.7 2.7 pad_maximum_fusion
  181.4 11.0 %all-to-all-done.5.grad_ref = bf16[32,128,128]{2,1,0:T(8,128)(2,1)S(1)} async-done(((bf16[32,128,128]{2,1,0:T(8,128)(2,1)}), bf16[32,128,128]{2,1,0:T(8,128)(2,1)S(1)}, u32[]{:S(2)}, u32[]{:S(2)}) %all-to-all-start.5) | async-done | bytes 1048608 | tf_op jit(solution)/shard_map/all_to_all | solution.py:255
  193.4 6.9 %all-to-all-start.4 = ((bf16[32,256,128]{2,1,0:T(8,128)(2,1)}), bf16[32,256,128]{2,1,0:T(8,128)(2,1)S(1)}, u32[]{:S(2)}, u32[]{:S(2)}) async-start(bf16[32,256,128]{2,1,0:T(8,128)(2,1)} %pad_maximum_fusion), calls=%async_computation.4 | async-start | bytes 4194304 | tf_op jit(solution)/shard_map/all_to_all | solution.py:255
  200.3 13.6 %tiles.1 = bf16[32,128,128]{2,1,0:T(8,128)(2,1)} custom-call(s32[1]{0:T(128)} %bitcast.lane_ref, bf16[32,128,128]{2,1,0:T(8,128)(2,1)} %copy-done.3, bf16[32,128,4096]{2,1,0:T(8,128)(2,1)} %bitcast.6), custom_call_target="tpu_custom_call" | custom-call | flops 4294967296 | bytes 35651584 | tf_op jit(solution)/shard_map/tiles/pallas_call | solution.py:205
  213.9 48.6 %reduce-scatter.2.cloned.1.call-done = bf16[1,512,128]{2,1,0:T(8,128)(2,1)} async-done(((bf16[8,512,128]{2,1,0:T(8,128)(2,1)}), bf16[1,512,128]{2,1,0:T(8,128)(2,1)}) %reduce-scatter.2.cloned.1.call-update) | async-done | bytes 131088 | tf_op jit(solution)/shard_map/reduce_scatter | solution.py:279
  262.5 4.6 %collective-permute-start = (bf16[512,128]{1,0:T(8,128)(2,1)}, bf16[512,128]{1,0:T(8,128)(2,1)S(1)}, u32[]{:S(2)}, u32[]{:S(2)}) collective-permute-start(bf16[512,128]{1,0:T(8,128)(2,1)} %bitcast.9), channel_id=1, source_target_pairs={{0,0},{1,1},{2,2},{3,3},{4,36},{5,37},{6,38},{7,39},{8,72},{9,73},... | collective-permute-start | bytes 393224 | tf_op jit(solution)/shard_map/ppermute | solution.py:282
  267.2 1.3 copy-done
  268.5 3.5 %unpack.1 = bf16[3,2,64,4096]{3,2,1,0:T(8,128)(2,1)} custom-call(bf16[32,64,128]{2,1,0:T(8,128)(2,1)} %copy-done.1, bf16[32,64,128]{2,1,0:T(8,128)(2,1)} %copy-done.2, bf16[32,256,128]{2,1,0:T(8,128)(2,1)} %copy-done), custom_call_target="tpu_custom_call" | custom-call | bytes 6291456 | tf_op jit(solution)/shard_map/unpack/pallas_call | solution.py:173
  272.0 1.5 collective-permute-done
  274.1 2.5 grams.1
  (20 shorter events, 2.5 us)
Async XLA Ops:
  7.2 193.1 %all-gather.2.cloned.1.call-start = ((), (), s32[]{:S(2)}) async-start(), calls=%async_computation.7 | async-start | bytes 34603008 | tf_op jit(solution)/shard_map/all_gather | solution.py:267
  10.6 60.2 %all-to-all-start = ((bf16[32,256,128]{2,1,0:T(8,128)(2,1)}), bf16[32,256,128]{2,1,0:T(8,128)(2,1)S(1)}, u32[]{:S(2)}, u32[]{:S(2)}) async-start(bf16[32,256,128]{2,1,0:T(8,128)(2,1)} %pack0.1), calls=%async_computation | async-start | bytes 4194304 | tf_op jit(solution)/shard_map/all_to_all | solution.py:255
  70.8 1.3 copy-start.5
  72.1 54.9 %all-to-all-start.2 = ((bf16[32,256,128]{2,1,0:T(8,128)(2,1)}), bf16[32,256,128]{2,1,0:T(8,128)(2,1)S(1)}, u32[]{:S(2)}, u32[]{:S(2)}) async-start(bf16[32,256,128]{2,1,0:T(8,128)(2,1)} %pack1.1), calls=%async_computation.2 | async-start | bytes 4194304 | tf_op jit(solution)/shard_map/all_to_all | solution.py:255
  127.0 4.4 %copy-start.4 = (bf16[32,256,128]{2,1,0:T(8,128)(2,1)}, bf16[32,256,128]{2,1,0:T(8,128)(2,1)S(1)}, u32[]{:S(2)}) copy-start(bf16[32,256,128]{2,1,0:T(8,128)(2,1)S(1)} %all-to-all-done.2.recv_ref) | copy-start | bytes 6291460
  127.0 21.2 %all-to-all-start.1 = ((bf16[32,64,128]{2,1,0:T(8,128)(2,1)}), bf16[32,64,128]{2,1,0:T(8,128)(2,1)S(1)}, u32[]{:S(2)}, u32[]{:S(2)}) async-start(bf16[32,64,128]{2,1,0:T(8,128)(2,1)} %get-tuple-element.9), calls=%async_computation.1 | async-start | bytes 1048576 | tf_op jit(solution)/shard_map/all_to_all | solution.py:255
  148.2 23.0 %copy-start.1 = (bf16[32,64,128]{2,1,0:T(8,128)(2,1)}, bf16[32,64,128]{2,1,0:T(8,128)(2,1)S(1)}, u32[]{:S(2)}) copy-start(bf16[32,64,128]{2,1,0:T(8,128)(2,1)S(1)} %all-to-all-done.1.q0_ref) | copy-start | bytes 1572868
  170.2 1.2 copy-start.2
  170.2 8.5 %copy-start.6 = (bf16[32,128,128]{2,1,0:T(8,128)(2,1)S(1)}, bf16[32,128,128]{2,1,0:T(8,128)(2,1)}, u32[]{:S(2)}) copy-start(bf16[32,128,128]{2,1,0:T(8,128)(2,1)} %get-tuple-element.11) | copy-start | bytes 3145732
  171.3 21.1 %all-to-all-start.5 = ((bf16[32,128,128]{2,1,0:T(8,128)(2,1)}), bf16[32,128,128]{2,1,0:T(8,128)(2,1)S(1)}, u32[]{:S(2)}, u32[]{:S(2)}) async-start(bf16[32,128,128]{2,1,0:T(8,128)(2,1)} %pad_maximum_fusion.1), calls=%async_computation.5 | async-start | bytes 2097152 | tf_op jit(solution)/shard_map/all_to_all | solution.py:255
  192.4 1.0 copy-start.3
  193.4 73.8 %all-to-all-start.4 = ((bf16[32,256,128]{2,1,0:T(8,128)(2,1)}), bf16[32,256,128]{2,1,0:T(8,128)(2,1)S(1)}, u32[]{:S(2)}, u32[]{:S(2)}) async-start(bf16[32,256,128]{2,1,0:T(8,128)(2,1)} %pad_maximum_fusion), calls=%async_computation.4 | async-start | bytes 4194304 | tf_op jit(solution)/shard_map/all_to_all | solution.py:255
  200.2 62.3 %reduce-scatter.2.cloned.1.call-start = ((), (), s32[]{:S(2)}) async-start(), calls=%async_computation.8 | async-start | bytes 1179648 | tf_op jit(solution)/shard_map/reduce_scatter | solution.py:279
  262.5 11.0 %collective-permute-start = (bf16[512,128]{1,0:T(8,128)(2,1)}, bf16[512,128]{1,0:T(8,128)(2,1)S(1)}, u32[]{:S(2)}, u32[]{:S(2)}) collective-permute-start(bf16[512,128]{1,0:T(8,128)(2,1)} %bitcast.9), channel_id=1, source_target_pairs={{0,0},{1,1},{2,2},{3,3},{4,36},{5,37},{6,38},{7,39},{8,72},{9,73},... | collective-permute-start | bytes 393224 | tf_op jit(solution)/shard_map/ppermute | solution.py:282
  267.2 1.3 copy-start
  273.5 0.6 copy-start.7
Sparse Core Ops, SparseCore 0:
  10.6 169.0 all-gather.1
  214.0 48.4 reduce-scatter.1

commit v4 on v3

--- a/solution.py
+++ b/solution.py
@@ -1,3 +1,4 @@
+import functools
 import math
 
 import jax
@@ -23,6 +24,7 @@
 BLOCK = 256
 PAD = 8
 VMEM = 60 << 20
+ANY = pl.BlockSpec(memory_space=pl.ANY)
 
 
 def nt_dot(a, b):
@@ -58,9 +60,11 @@
     )(qkv_pre, d_out)
 
 
-def attention_kernel(
-    recv_ref, taps_ref, gq_ref, gkv_ref, pad_ref, post_ref, kt_ref, s_ref, w_ref, grad_ref
-):
+def attention_kernel(seq, recv_ref, taps_ref, *rest):
+    *refs, pad_ref, post_ref, kt_ref, s_ref, w_ref, grad_ref = rest
+    gq_ref, gkv_ref = refs[-2:]
+    if seq == 1:
+        gq_ref[:, 0:TOK, :] = refs[0][...]
     scale = 1.0 / math.sqrt(HDIM)
     factor = scale * math.log2(math.e)
     pad_ref[0:PAD, :] = jnp.zeros((PAD, HDIM), jnp.float32)
@@ -86,31 +90,33 @@
         d_out = recv_ref[i * per_block : (i + 1) * per_block, 3 * TOK : 4 * TOK, :].reshape(
             BLOCK, HDIM
         )
-        top = None
+        tops, total, inner = [], None, None
         for j in range(i + 1):
             cols = slice(j * BLOCK, (j + 1) * BLOCK)
             scores = nt_dot(post_ref[1, cols, :], query)
+            weights = nt_dot(post_ref[2, cols, :], d_out)
             if j == i:
                 scores = jnp.where(key_ids <= query_ids, scores, -jnp.inf)
-            s_ref[cols, :] = scores
-            part = jnp.max(scores, axis=0, keepdims=True)
-            top = part if top is None else jnp.maximum(top, part)
-        total = jnp.zeros((1, BLOCK), jnp.float32)
-        inner = jnp.zeros((1, BLOCK), jnp.float32)
-        for j in range(i + 1):
-            cols = slice(j * BLOCK, (j + 1) * BLOCK)
-            exponent = jnp.exp2((s_ref[cols, :] - top) * factor)
-            weights = nt_dot(post_ref[2, cols, :], d_out)
+            top = jnp.max(scores, axis=0, keepdims=True)
+            if j > 0:
+                top = jnp.maximum(tops[-1], top)
+            exponent = jnp.exp2((scores - top) * factor)
             s_ref[cols, :] = exponent
             w_ref[cols, :] = weights
-            total = total + jnp.sum(exponent, axis=0, keepdims=True)
-            inner = inner + jnp.sum(exponent * weights, axis=0, keepdims=True)
+            sum_e = jnp.sum(exponent, axis=0, keepdims=True)
+            sum_w = jnp.sum(exponent * weights, axis=0, keepdims=True)
+            if j == 0:
+                total, inner = sum_e, sum_w
+            else:
+                shrink = jnp.exp2((tops[-1] - top) * factor)
+                total, inner = total * shrink + sum_e, inner * shrink + sum_w
+            tops.append(top)
         inverse = 1.0 / total
         inner = inner * inverse
         dq_t = jnp.zeros((HDIM, BLOCK), jnp.float32)
         for j in range(i + 1):
             cols = slice(j * BLOCK, (j + 1) * BLOCK)
-            prob = s_ref[cols, :] * inverse
+            prob = s_ref[cols, :] * (jnp.exp2((tops[j] - tops[i]) * factor) * inverse)
             d_scores = (prob * (w_ref[cols, :] - inner)).astype(jnp.bfloat16)
             grad_ref[1, cols, :] += nn_dot(d_scores, query)
             grad_ref[2, cols, :] += nn_dot(prob.astype(jnp.bfloat16), d_out)
@@ -126,19 +132,19 @@
         )
         halves = grads.astype(jnp.bfloat16).reshape(N_CTX, TOK, HDIM)
         if j == 0:
-            gq_ref[...] = halves
+            gq_ref[:, seq * TOK : (seq + 1) * TOK, :] = halves
         else:
             gkv_ref[:, (j - 1) * TOK : j * TOK, :] = halves
 
 
-def attention(received, taps, seq):
+def attention(received, taps, seq, *early):
     vmem = pl.BlockSpec(memory_space=pltpu.VMEM)
     return pl.pallas_call(
-        attention_kernel,
-        in_specs=[vmem, vmem],
+        functools.partial(attention_kernel, seq),
+        in_specs=[vmem] * (2 + len(early)),
         out_specs=[vmem, vmem],
         out_shape=[
-            jax.ShapeDtypeStruct((N_CTX, TOK, HDIM), jnp.bfloat16),
+            jax.ShapeDtypeStruct((N_CTX, (1 + seq) * TOK, HDIM), jnp.bfloat16),
             jax.ShapeDtypeStruct((N_CTX, 2 * TOK, HDIM), jnp.bfloat16),
         ],
         scratch_shapes=[
@@ -154,32 +160,48 @@
         cost_estimate=pl.CostEstimate(
             flops=6 * LEN * LEN * HDIM, bytes_accessed=4 << 20, transcendentals=LEN * LEN // 2
         ),
-    )(received, taps)
-
-
-def unpack_kernel(q0_ref, q1_ref, kv_ref, out_ref):
-    for c in range(q0_ref.shape[0]):
+    )(received, taps, *early)
+
+
+def after_kernel(*refs):
+    pass
+
+
+def after(value, *others):
+    return pl.pallas_call(
+        after_kernel,
+        in_specs=[ANY] * (1 + len(others)),
+        out_specs=ANY,
+        out_shape=jax.ShapeDtypeStruct(value.shape, value.dtype),
+        input_output_aliases={0: 0},
+        name="after",
+    )(value, *others)
+
+
+def unpack_kernel(q_ref, kv_ref, out_ref):
+    for c in range(q_ref.shape[0]):
         lanes = slice(c * HDIM, (c + 1) * HDIM)
-        for seq, q_ref in enumerate((q0_ref, q1_ref)):
+        for seq in range(2):
             first = 2 * seq * TOK
-            out_ref[0, seq, :, lanes] = q_ref[c]
+            out_ref[0, seq, :, lanes] = q_ref[c, seq * TOK : (seq + 1) * TOK, :]
             out_ref[1, seq, :, lanes] = kv_ref[c, first : first + TOK, :]
             out_ref[2, seq, :, lanes] = kv_ref[c, first + TOK : first + 2 * TOK, :]
 
 
-def unpack(q0, q1, kv, width=16):
-    q_spec = pl.BlockSpec((width, TOK, HDIM), lambda i: (i, 0, 0))
-    kv_spec = pl.BlockSpec((width, 4 * TOK, HDIM), lambda i: (i, 0, 0))
+def unpack(q, kv, width=16):
     return pl.pallas_call(
         unpack_kernel,
         grid=(N_CTX // width,),
-        in_specs=[q_spec, q_spec, kv_spec],
+        in_specs=[
+            pl.BlockSpec((width, 2 * TOK, HDIM), lambda i: (i, 0, 0)),
+            pl.BlockSpec((width, 4 * TOK, HDIM), lambda i: (i, 0, 0)),
+        ],
         out_specs=pl.BlockSpec((3, 2, TOK, width * HDIM), lambda i: (0, 0, 0, i)),
         out_shape=jax.ShapeDtypeStruct((3, 2, TOK, N_CTX * HDIM), jnp.bfloat16),
-        compiler_params=pltpu.CompilerParams(vmem_limit_bytes=VMEM),
+        compiler_params=pltpu.CompilerParams(vmem_limit_bytes=24 << 20),
         name="unpack",
         cost_estimate=pl.CostEstimate(flops=0, bytes_accessed=6 << 20, transcendentals=0),
-    )(q0, q1, kv)
+    )(q, kv)
 
 
 FEATS = 1024
@@ -268,11 +290,12 @@
     gathered = gathered.reshape(N_CTX, 2 * TOK, N_CTX * HDIM)
 
     received = [swap(pack(qkv_pre, d_out, seq), CTX) for seq in range(2)]
-    gq, gkv = zip(*[attention(received[seq], conv_taps, seq) for seq in range(2)])
-    gq = [swap(part, CTX) for part in gq]
-    columns = swap(jnp.concatenate(gq, axis=1), PLANE)
-    gkv = swap(jnp.concatenate(gkv, axis=1), CTX)
-    grad_qkv = unpack(gq[0], gq[1], gkv)
+    query0, kv0 = attention(received[0], conv_taps, 0)
+    query, kv1 = attention(received[1], conv_taps, 1, query0)
+    query = swap(query, CTX)
+    columns = swap(query, PLANE)
+    keys_values = swap(jnp.concatenate([kv0, kv1], axis=1), CTX)
+    grad_qkv = unpack(query, keys_values)
 
     lane = (lax.axis_index("yl") * 2 + lax.axis_index("core")).astype(jnp.int32).reshape(1)
     partial = tile_sums(columns, gathered, lane)
@@ -280,6 +303,7 @@
         partial.reshape(N_Z, SPAN * HDIM, HDIM), "z", scatter_dimension=0, tiled=True
     )[0]
     tiles = lax.ppermute(summed, ALL, owner_pairs()).reshape(SPAN, HDIM, HDIM)
+    tiles = after(tiles, grad_qkv)
     new_left, new_right = grams(tiles, left_old, right_old)
     return (grad_qkv, new_left, new_right)
 

time: 284 us -> 284 us (level)
  blocking collectives: 21.9 us -> 32.7 us
  starting transfers between devices: 37.3 us -> 32.8 us
  local copies, waits for them, and re-layouts: 4.35 us -> 0.66 us
    all_to_all x1, blocking collectives: 21.9 us -> 32.7 us  [swap(): return lax.all_to_all(value, axes, split_axis=0, concat_axis=0, tiled=True)]
    all_to_all x5 -> x4, starting transfers between devices: 32.6 us -> 28.2 us  [swap(): return lax.all_to_all(value, axes, split_axis=0, concat_axis=0, tiled=True)]
    unnamed x16 -> x10, local copies, waits for them, and re-layouts: 4.35 us -> 0.66 us
    all_to_all x5 -> x4, waiting for transfers between devices: 99 us -> 97.2 us  [swap(): return lax.all_to_all(value, axes, split_axis=0, concat_axis=0, tiled=True)]
    pallas_call x3 -> x4, Pallas kernels: 30.7 us -> 29.7 us  [the longest x2 26.5 us: attention(): pl.pallas_call(functools.partial(attention_kernel, seq), in_specs=[vmem]...]
  transfers between devices with their start and end apart: 8 -> 7, of which waited for: 6 -> 5; matrix products, arithmetic and copies ran while one was open for 1% -> 1% of each run, Pallas kernels for 18% -> 17%
where the time goes in v4:
time: 284 us; the launch traced here: 283 us
  waiting for transfers between devices  150 us (53%)
  Pallas kernels  51.2 us (18%)
  starting transfers between devices  32.8 us (12%)
  blocking collectives  32.7 us (12%)
  between operations  14.1 us (5%)
    all_to_all x4, waiting for transfers between devices, swap(): return lax.all_to_all(value, axes, split_axis=0, concat_axis=0, tiled=True)  97.2 us
    reduce_scatter x1, waiting for transfers between devices, on_device(): lax.psum_scatter(partial.reshape(N_Z, SPAN * HDIM, HDIM), 'z', scatter_di...  48.7 us
    all_to_all x1, blocking collectives, swap(): return lax.all_to_all(value, axes, split_axis=0, concat_axis=0, tiled=True)  32.7 us
    all_to_all x4, starting transfers between devices, swap(): return lax.all_to_all(value, axes, split_axis=0, concat_axis=0, tiled=True)  28.2 us
    pallas_call x2, Pallas kernels, attention(): pl.pallas_call(functools.partial(attention_kernel, seq), in_specs=[vmem]...  26.5 us
    pallas_call x1, Pallas kernels, tile_sums(): pl.pallas_call(tiles_kernel, grid=(N_CTX * HDIM // FEATS,), in_specs=[pl....  13.6 us
  transfers between devices with their start and end apart: 7, of which 5 were waited for; matrix products, arithmetic and copies ran while one was open for 1% of the time, Pallas kernels for 17%

profile of v4, /device:TPU:46, one launch (start us, length us, event | category | flops | bytes accessed | tf_op | source)
XLA Modules:
  0.0 282.9 jit_solution(1071805435428273174)
XLA Ops:
  7.2 0.0 all-gather.2.cloned.1.call-start
  7.2 0.7 all-gather.2.cloned.1.call-update
  7.9 2.7 pack0.1
  10.6 9.6 %all-to-all-start.1 = ((bf16[32,256,128]{2,1,0:T(8,128)(2,1)}), bf16[32,256,128]{2,1,0:T(8,128)(2,1)S(1)}, u32[]{:S(2)}, u32[]{:S(2)}) async-start(bf16[32,256,128]{2,1,0:T(8,128)(2,1)} %pack0.1), calls=%async_computation.1 | async-start | bytes 4194304 | tf_op jit(solution)/shard_map/all_to_all | solution.py:277
  20.2 2.7 pack1.1
  22.9 47.8 %all-to-all-done.1.recv_ref = bf16[32,256,128]{2,1,0:T(8,128)(2,1)S(1)} async-done(((bf16[32,256,128]{2,1,0:T(8,128)(2,1)}), bf16[32,256,128]{2,1,0:T(8,128)(2,1)S(1)}, u32[]{:S(2)}, u32[]{:S(2)}) %all-to-all-start.1) | async-done | bytes 2097184 | tf_op jit(solution)/shard_map/all_to_all | solution.py:277
  70.8 4.6 %all-to-all-start = ((bf16[32,256,128]{2,1,0:T(8,128)(2,1)}), bf16[32,256,128]{2,1,0:T(8,128)(2,1)}, u32[]{:S(2)}, u32[]{:S(2)}) async-start(bf16[32,256,128]{2,1,0:T(8,128)(2,1)} %pack1.1), calls=%async_computation | async-start | bytes 4194304 | tf_op jit(solution)/shard_map/all_to_all | solution.py:277
  75.3 13.4 %attention0.1 = (bf16[32,64,128]{2,1,0:T(8,128)(2,1)}, bf16[32,128,128]{2,1,0:T(8,128)(2,1)}) custom-call(bf16[32,256,128]{2,1,0:T(8,128)(2,1)} %copy-done.1, f32[3,3,128]{2,1,0:T(4,128)} %taps_ref.3), custom_call_target="tpu_custom_call" | custom-call | flops 3221225472 | bytes 4194304 | tf_op jit(solution)/shard_map/attention0/pallas_call | solution.py:142
  88.7 37.1 %all-to-all-done.recv_ref = bf16[32,256,128]{2,1,0:T(8,128)(2,1)} async-done(((bf16[32,256,128]{2,1,0:T(8,128)(2,1)}), bf16[32,256,128]{2,1,0:T(8,128)(2,1)}, u32[]{:S(2)}, u32[]{:S(2)}) %all-to-all-start) | async-done | bytes 2097184 | tf_op jit(solution)/shard_map/all_to_all | solution.py:277
  125.9 13.2 %attention1.1 = (bf16[32,128,128]{2,1,0:T(8,128)(2,1)}, bf16[32,128,128]{2,1,0:T(8,128)(2,1)}) custom-call(bf16[32,256,128]{2,1,0:T(8,128)(2,1)} %all-to-all-done.recv_ref, f32[3,3,128]{2,1,0:T(4,128)} %taps_ref.3, bf16[32,64,128]{2,1,0:T(8,128)(2,1)} %get-tuple-element.9.rest_0_), custom_call_target="tpu_custom_call" | custom-call | flops 3221225472 | bytes 4194304 | tf_op jit(solution)/shard_map/attention1/pallas_call | solution.py:142
  139.0 32.7 %all_to_all.25.q_ref = bf16[32,128,128]{2,1,0:T(8,128)(2,1)} all-to-all(bf16[32,128,128]{2,1,0:T(8,128)(2,1)} %get-tuple-element.10), channel_id=1, replica_groups=mesh['x'=4,'yh'=2,'z'=8,'yl'=2,'core'=2] {'z','yl','core'}, dimensions={0} | all-to-all | bytes 2097152 | tf_op jit(solution)/shard_map/all_to_all | solution.py:277
  171.8 7.4 %all-to-all-start.4 = ((bf16[32,128,128]{2,1,0:T(8,128)(2,1)}), bf16[32,128,128]{2,1,0:T(8,128)(2,1)S(1)}, u32[]{:S(2)}, u32[]{:S(2)}) async-start(bf16[32,128,128]{2,1,0:T(8,128)(2,1)} %all_to_all.25.q_ref), calls=%async_computation.4 | async-start | bytes 2097152 | tf_op jit(solution)/shard_map/all_to_all | solution.py:277
  179.2 1.5 pad_maximum_fusion
  180.6 12.3 %all-to-all-done.4.grad_ref = bf16[32,128,128]{2,1,0:T(8,128)(2,1)S(1)} async-done(((bf16[32,128,128]{2,1,0:T(8,128)(2,1)}), bf16[32,128,128]{2,1,0:T(8,128)(2,1)S(1)}, u32[]{:S(2)}, u32[]{:S(2)}) %all-to-all-start.4) | async-done | bytes 1048608 | tf_op jit(solution)/shard_map/all_to_all | solution.py:277
  192.9 6.7 %all-to-all-start.3 = ((bf16[32,256,128]{2,1,0:T(8,128)(2,1)}), bf16[32,256,128]{2,1,0:T(8,128)(2,1)S(1)}, u32[]{:S(2)}, u32[]{:S(2)}) async-start(bf16[32,256,128]{2,1,0:T(8,128)(2,1)} %pad_maximum_fusion), calls=%async_computation.3 | async-start | bytes 4194304 | tf_op jit(solution)/shard_map/all_to_all | solution.py:277
  199.5 0.0 reduce-scatter.2.cloned.1.call-start
  199.6 0.0 all-gather.2.cloned.1.call-done
  199.6 13.6 %tiles.1 = bf16[32,128,128]{2,1,0:T(8,128)(2,1)} custom-call(s32[1]{0:T(128)} %bitcast.lane_ref, bf16[32,128,128]{2,1,0:T(8,128)(2,1)} %copy-done, bf16[32,128,4096]{2,1,0:T(8,128)(2,1)} %bitcast.6), custom_call_target="tpu_custom_call" | custom-call | flops 4294967296 | bytes 35651584 | tf_op jit(solution)/shard_map/tiles/pallas_call | solution.py:227
  213.2 48.7 %reduce-scatter.2.cloned.1.call-done = bf16[1,512,128]{2,1,0:T(8,128)(2,1)} async-done(((bf16[8,512,128]{2,1,0:T(8,128)(2,1)}), bf16[1,512,128]{2,1,0:T(8,128)(2,1)}) %reduce-scatter.2.cloned.1.call-update) | async-done | bytes 131088 | tf_op jit(solution)/shard_map/reduce_scatter | solution.py:302
  261.9 4.5 %collective-permute-start = (bf16[512,128]{1,0:T(8,128)(2,1)}, bf16[512,128]{1,0:T(8,128)(2,1)S(1)}, u32[]{:S(2)}, u32[]{:S(2)}) collective-permute-start(bf16[512,128]{1,0:T(8,128)(2,1)} %bitcast.10), channel_id=1, source_target_pairs={{0,0},{1,1},{2,2},{3,3},{4,36},{5,37},{6,38},{7,39},{8,72},{9,73},... | collective-permute-start | bytes 393224 | tf_op jit(solution)/shard_map/ppermute | solution.py:305
  266.4 3.2 %unpack.1.refs_1_ = bf16[3,2,64,4096]{3,2,1,0:T(8,128)(2,1)} custom-call(bf16[32,128,128]{2,1,0:T(8,128)(2,1)} %all_to_all.25.q_ref, bf16[32,256,128]{2,1,0:T(8,128)(2,1)S(1)} %all-to-all-done.3.kv_ref), custom_call_target="tpu_custom_call" | custom-call | bytes 6291456 | tf_op jit(solution)/shard_map/unpack/pallas_call | solution.py:192
  269.6 3.3 %collective-permute-done = bf16[512,128]{1,0:T(8,128)(2,1)S(1)} collective-permute-done((bf16[512,128]{1,0:T(8,128)(2,1)}, bf16[512,128]{1,0:T(8,128)(2,1)S(1)}, u32[]{:S(2)}, u32[]{:S(2)}) %collective-permute-start) | collective-permute-done | bytes 131104 | tf_op jit(solution)/shard_map/ppermute | solution.py:305
  272.9 0.6 copy-done.4
  273.5 2.5 grams.1
  (12 shorter events, 0.0 us)
Async XLA Ops:
  7.2 192.5 %all-gather.2.cloned.1.call-start = ((), (), s32[]{:S(2)}) async-start(), calls=%async_computation.6 | async-start | bytes 34603008 | tf_op jit(solution)/shard_map/all_gather | solution.py:289
  10.6 60.2 %all-to-all-start.1 = ((bf16[32,256,128]{2,1,0:T(8,128)(2,1)}), bf16[32,256,128]{2,1,0:T(8,128)(2,1)S(1)}, u32[]{:S(2)}, u32[]{:S(2)}) async-start(bf16[32,256,128]{2,1,0:T(8,128)(2,1)} %pack0.1), calls=%async_computation.1 | async-start | bytes 4194304 | tf_op jit(solution)/shard_map/all_to_all | solution.py:277
  70.8 4.6 %copy-start.1 = (bf16[32,256,128]{2,1,0:T(8,128)(2,1)}, bf16[32,256,128]{2,1,0:T(8,128)(2,1)S(1)}, u32[]{:S(2)}) copy-start(bf16[32,256,128]{2,1,0:T(8,128)(2,1)S(1)} %all-to-all-done.1.recv_ref) | copy-start | bytes 6291460
  70.8 55.1 %all-to-all-start = ((bf16[32,256,128]{2,1,0:T(8,128)(2,1)}), bf16[32,256,128]{2,1,0:T(8,128)(2,1)}, u32[]{:S(2)}, u32[]{:S(2)}) async-start(bf16[32,256,128]{2,1,0:T(8,128)(2,1)} %pack1.1), calls=%async_computation | async-start | bytes 4194304 | tf_op jit(solution)/shard_map/all_to_all | solution.py:277
  139.0 40.1 %copy-start.2 = (bf16[32,128,128]{2,1,0:T(8,128)(2,1)S(1)}, bf16[32,128,128]{2,1,0:T(8,128)(2,1)}, u32[]{:S(2)}) copy-start(bf16[32,128,128]{2,1,0:T(8,128)(2,1)} %get-tuple-element.11) | copy-start | bytes 3145732
  139.0 40.1 %copy-start.3 = (bf16[32,128,128]{2,1,0:T(8,128)(2,1)S(1)}, bf16[32,128,128]{2,1,0:T(8,128)(2,1)}, u32[]{:S(2)}) copy-start(bf16[32,128,128]{2,1,0:T(8,128)(2,1)} %get-tuple-element.12) | copy-start | bytes 3145732
  171.8 21.1 %all-to-all-start.4 = ((bf16[32,128,128]{2,1,0:T(8,128)(2,1)}), bf16[32,128,128]{2,1,0:T(8,128)(2,1)S(1)}, u32[]{:S(2)}, u32[]{:S(2)}) async-start(bf16[32,128,128]{2,1,0:T(8,128)(2,1)} %all_to_all.25.q_ref), calls=%async_computation.4 | async-start | bytes 2097152 | tf_op jit(solution)/shard_map/all_to_all | solution.py:277
  192.9 6.7 %copy-start = (bf16[32,128,128]{2,1,0:T(8,128)(2,1)}, bf16[32,128,128]{2,1,0:T(8,128)(2,1)S(1)}, u32[]{:S(2)}) copy-start(bf16[32,128,128]{2,1,0:T(8,128)(2,1)S(1)} %all-to-all-done.4.grad_ref) | copy-start | bytes 3145732
  192.9 73.5 %all-to-all-start.3 = ((bf16[32,256,128]{2,1,0:T(8,128)(2,1)}), bf16[32,256,128]{2,1,0:T(8,128)(2,1)S(1)}, u32[]{:S(2)}, u32[]{:S(2)}) async-start(bf16[32,256,128]{2,1,0:T(8,128)(2,1)} %pad_maximum_fusion), calls=%async_computation.3 | async-start | bytes 4194304 | tf_op jit(solution)/shard_map/all_to_all | solution.py:277
  199.5 62.4 %reduce-scatter.2.cloned.1.call-start = ((), (), s32[]{:S(2)}) async-start(), calls=%async_computation.7 | async-start | bytes 1179648 | tf_op jit(solution)/shard_map/reduce_scatter | solution.py:302
  261.9 11.0 %collective-permute-start = (bf16[512,128]{1,0:T(8,128)(2,1)}, bf16[512,128]{1,0:T(8,128)(2,1)S(1)}, u32[]{:S(2)}, u32[]{:S(2)}) collective-permute-start(bf16[512,128]{1,0:T(8,128)(2,1)} %bitcast.10), channel_id=1, source_target_pairs={{0,0},{1,1},{2,2},{3,3},{4,36},{5,37},{6,38},{7,39},{8,72},{9,73},... | collective-permute-start | bytes 393224 | tf_op jit(solution)/shard_map/ppermute | solution.py:305
  272.9 0.6 copy-start.4
Sparse Core Ops, SparseCore 0:
  10.6 169.0 all-gather.1
  213.3 48.5 reduce-scatter.1

commit v5 on v4

--- a/solution.py
+++ b/solution.py
@@ -178,30 +178,27 @@
     )(value, *others)
 
 
-def unpack_kernel(q_ref, kv_ref, out_ref):
+def unpack_kernel(q_ref, kv0_ref, kv1_ref, out_ref):
     for c in range(q_ref.shape[0]):
         lanes = slice(c * HDIM, (c + 1) * HDIM)
-        for seq in range(2):
-            first = 2 * seq * TOK
+        for seq, kv_ref in enumerate((kv0_ref, kv1_ref)):
             out_ref[0, seq, :, lanes] = q_ref[c, seq * TOK : (seq + 1) * TOK, :]
-            out_ref[1, seq, :, lanes] = kv_ref[c, first : first + TOK, :]
-            out_ref[2, seq, :, lanes] = kv_ref[c, first + TOK : first + 2 * TOK, :]
-
-
-def unpack(q, kv, width=16):
+            out_ref[1, seq, :, lanes] = kv_ref[c, 0:TOK, :]
+            out_ref[2, seq, :, lanes] = kv_ref[c, TOK : 2 * TOK, :]
+
+
+def unpack(q, kv0, kv1, width=16):
+    spec = pl.BlockSpec((width, 2 * TOK, HDIM), lambda i: (i, 0, 0))
     return pl.pallas_call(
         unpack_kernel,
         grid=(N_CTX // width,),
-        in_specs=[
-            pl.BlockSpec((width, 2 * TOK, HDIM), lambda i: (i, 0, 0)),
-            pl.BlockSpec((width, 4 * TOK, HDIM), lambda i: (i, 0, 0)),
-        ],
+        in_specs=[spec] * 3,
         out_specs=pl.BlockSpec((3, 2, TOK, width * HDIM), lambda i: (0, 0, 0, i)),
         out_shape=jax.ShapeDtypeStruct((3, 2, TOK, N_CTX * HDIM), jnp.bfloat16),
         compiler_params=pltpu.CompilerParams(vmem_limit_bytes=24 << 20),
         name="unpack",
         cost_estimate=pl.CostEstimate(flops=0, bytes_accessed=6 << 20, transcendentals=0),
-    )(q, kv)
+    )(q, kv0, kv1)
 
 
 FEATS = 1024
@@ -294,8 +291,9 @@
     query, kv1 = attention(received[1], conv_taps, 1, query0)
     query = swap(query, CTX)
     columns = swap(query, PLANE)
-    keys_values = swap(jnp.concatenate([kv0, kv1], axis=1), CTX)
-    grad_qkv = unpack(query, keys_values)
+    kv0 = swap(kv0, CTX)
+    kv1 = swap(after(kv1, kv0), CTX)
+    grad_qkv = unpack(query, kv0, kv1)
 
     lane = (lax.axis_index("yl") * 2 + lax.axis_index("core")).astype(jnp.int32).reshape(1)
     partial = tile_sums(columns, gathered, lane)

time: 284 us -> 281 us (0.989)
  waiting for transfers between devices: 150 us -> 129 us
  blocking collectives: 32.7 us -> 53.5 us
    reduce_scatter x1, waiting for transfers between devices: 48.7 us -> 24.9 us  [on_device(): lax.psum_scatter(partial.reshape(N_Z, SPAN * HDIM, HDIM), 'z', scatter_di...]
    all_to_all x1 -> x2, blocking collectives: 32.7 us -> 53.5 us  [swap(): return lax.all_to_all(value, axes, split_axis=0, concat_axis=0, tiled=True)]
    all_to_all x4, waiting for transfers between devices: 97.2 us -> 102 us  [swap(): return lax.all_to_all(value, axes, split_axis=0, concat_axis=0, tiled=True)]
  transfers between devices with their start and end apart: 7 -> 7, of which waited for: 5 -> 6; matrix products, arithmetic and copies ran while one was open for 1% -> 0% of each run, Pallas kernels for 17% -> 17%
where the time goes in v5:
time: 281 us; the launch traced here: 279 us
  waiting for transfers between devices  129 us (46%)
  blocking collectives  53.5 us (19%)
  Pallas kernels  50.2 us (18%)
  starting transfers between devices  31 us (11%)
  between operations  14.1 us (5%)
    all_to_all x4, waiting for transfers between devices, swap(): return lax.all_to_all(value, axes, split_axis=0, concat_axis=0, tiled=True)  102 us
    all_to_all x2, blocking collectives, swap(): return lax.all_to_all(value, axes, split_axis=0, concat_axis=0, tiled=True)  53.5 us
    pallas_call x2, Pallas kernels, attention(): pl.pallas_call(functools.partial(attention_kernel, seq), in_specs=[vmem]...  26.5 us
    all_to_all x4, starting transfers between devices, swap(): return lax.all_to_all(value, axes, split_axis=0, concat_axis=0, tiled=True)  25.9 us
    reduce_scatter x1, waiting for transfers between devices, on_device(): lax.psum_scatter(partial.reshape(N_Z, SPAN * HDIM, HDIM), 'z', scatter_di...  24.9 us
    pallas_call x1, Pallas kernels, tile_sums(): pl.pallas_call(tiles_kernel, grid=(N_CTX * HDIM // FEATS,), in_specs=[pl....  13.6 us
  transfers between devices with their start and end apart: 7, of which 6 were waited for; matrix products, arithmetic and copies ran while one was open for 0% of the time, Pallas kernels for 17%

profile of v5, /device:TPU:46, one launch (start us, length us, event | category | flops | bytes accessed | tf_op | source)
XLA Modules:
  0.0 279.3 jit_solution(11057367585312042533)
XLA Ops:
  7.2 0.7 all-gather.2.cloned.1.call-update
  7.9 2.7 pack0.1
  10.6 9.6 %all-to-all-start.1 = ((bf16[32,256,128]{2,1,0:T(8,128)(2,1)}), bf16[32,256,128]{2,1,0:T(8,128)(2,1)S(1)}, u32[]{:S(2)}, u32[]{:S(2)}) async-start(bf16[32,256,128]{2,1,0:T(8,128)(2,1)} %pack0.1), calls=%async_computation.1 | async-start | bytes 4194304 | tf_op jit(solution)/shard_map/all_to_all | solution.py:274
  20.2 2.7 pack1.1
  23.0 47.8 %all-to-all-done.1.recv_ref = bf16[32,256,128]{2,1,0:T(8,128)(2,1)S(1)} async-done(((bf16[32,256,128]{2,1,0:T(8,128)(2,1)}), bf16[32,256,128]{2,1,0:T(8,128)(2,1)S(1)}, u32[]{:S(2)}, u32[]{:S(2)}) %all-to-all-start.1) | async-done | bytes 2097184 | tf_op jit(solution)/shard_map/all_to_all | solution.py:274
  70.8 4.5 %all-to-all-start = ((bf16[32,256,128]{2,1,0:T(8,128)(2,1)}), bf16[32,256,128]{2,1,0:T(8,128)(2,1)}, u32[]{:S(2)}, u32[]{:S(2)}) async-start(bf16[32,256,128]{2,1,0:T(8,128)(2,1)} %pack1.1), calls=%async_computation | async-start | bytes 4194304 | tf_op jit(solution)/shard_map/all_to_all | solution.py:274
  75.3 13.4 %attention0.1 = (bf16[32,64,128]{2,1,0:T(8,128)(2,1)}, bf16[32,128,128]{2,1,0:T(8,128)(2,1)}) custom-call(bf16[32,256,128]{2,1,0:T(8,128)(2,1)} %copy-done.2, f32[3,3,128]{2,1,0:T(4,128)} %taps_ref.3), custom_call_target="tpu_custom_call" | custom-call | flops 3221225472 | bytes 4194304 | tf_op jit(solution)/shard_map/attention0/pallas_call | solution.py:142
  88.7 37.1 %all-to-all-done.recv_ref = bf16[32,256,128]{2,1,0:T(8,128)(2,1)} async-done(((bf16[32,256,128]{2,1,0:T(8,128)(2,1)}), bf16[32,256,128]{2,1,0:T(8,128)(2,1)}, u32[]{:S(2)}, u32[]{:S(2)}) %all-to-all-start) | async-done | bytes 2097184 | tf_op jit(solution)/shard_map/all_to_all | solution.py:274
  125.9 13.2 %attention1.1 = (bf16[32,128,128]{2,1,0:T(8,128)(2,1)}, bf16[32,128,128]{2,1,0:T(8,128)(2,1)}) custom-call(bf16[32,256,128]{2,1,0:T(8,128)(2,1)} %all-to-all-done.recv_ref, f32[3,3,128]{2,1,0:T(4,128)} %taps_ref.3, bf16[32,64,128]{2,1,0:T(8,128)(2,1)} %get-tuple-element.9.rest_0_), custom_call_target="tpu_custom_call" | custom-call | flops 3221225472 | bytes 4194304 | tf_op jit(solution)/shard_map/attention1/pallas_call | solution.py:142
  139.0 32.5 %all_to_all.30.q_ref = bf16[32,128,128]{2,1,0:T(8,128)(2,1)S(1)} all-to-all(bf16[32,128,128]{2,1,0:T(8,128)(2,1)} %get-tuple-element.10), channel_id=1, replica_groups=mesh['x'=4,'yh'=2,'z'=8,'yl'=2,'core'=2] {'z','yl','core'}, dimensions={0} | all-to-all | bytes 2097152 | tf_op jit(solution)/shard_map/all_to_all | solution.py:274
  171.5 21.0 %all_to_all.31.grad_ref = bf16[32,128,128]{2,1,0:T(8,128)(2,1)} all-to-all(bf16[32,128,128]{2,1,0:T(8,128)(2,1)S(1)} %all_to_all.30.q_ref), channel_id=1, replica_groups=mesh['x'=4,'yh'=2,'z'=8,'yl'=2,'core'=2] {'x','yh','yl','core'}, dimensions={0} | all-to-all | bytes 2097152 | tf_op jit(solution)/shard_map/all_to_all | solution.py:274
  192.5 6.6 %all-to-all-start.3 = ((bf16[32,128,128]{2,1,0:T(8,128)(2,1)}), bf16[32,128,128]{2,1,0:T(8,128)(2,1)S(1)}, u32[]{:S(2)}, u32[]{:S(2)}) async-start(bf16[32,128,128]{2,1,0:T(8,128)(2,1)} %get-tuple-element.11), calls=%async_computation.3 | async-start | bytes 2097152 | tf_op jit(solution)/shard_map/all_to_all | solution.py:274
  199.1 0.0 reduce-scatter.2.cloned.1.call-start
  199.2 13.6 %tiles.1 = bf16[32,128,128]{2,1,0:T(8,128)(2,1)} custom-call(s32[1]{0:T(128)} %bitcast.lane_ref, bf16[32,128,128]{2,1,0:T(8,128)(2,1)} %all_to_all.31.grad_ref, bf16[32,128,4096]{2,1,0:T(8,128)(2,1)} %bitcast.6), custom_call_target="tpu_custom_call" | custom-call | flops 4294967296 | bytes 35651584 | tf_op jit(solution)/shard_map/tiles/pallas_call | solution.py:224
  212.8 14.5 %all-to-all-done.3.refs_1_.kv0_ref = bf16[32,128,128]{2,1,0:T(8,128)(2,1)S(1)} async-done(((bf16[32,128,128]{2,1,0:T(8,128)(2,1)}), bf16[32,128,128]{2,1,0:T(8,128)(2,1)S(1)}, u32[]{:S(2)}, u32[]{:S(2)}) %all-to-all-start.3) | async-done | bytes 1048608 | tf_op jit(solution)/shard_map/all_to_all | solution.py:274
  227.3 1.0 copy-done
  228.2 5.1 %all-to-all-start.4 = ((bf16[32,128,128]{2,1,0:T(8,128)(2,1)}), bf16[32,128,128]{2,1,0:T(8,128)(2,1)S(1)}, u32[]{:S(2)}, u32[]{:S(2)}) async-start(bf16[32,128,128]{2,1,0:T(8,128)(2,1)} %after.2), calls=%async_computation.4 | async-start | bytes 2097152 | tf_op jit(solution)/shard_map/all_to_all | solution.py:274
  233.4 24.9 %reduce-scatter.2.cloned.1.call-done = bf16[1,512,128]{2,1,0:T(8,128)(2,1)} async-done(((bf16[8,512,128]{2,1,0:T(8,128)(2,1)}), bf16[1,512,128]{2,1,0:T(8,128)(2,1)}) %reduce-scatter.2.cloned.1.call-update) | async-done | bytes 131088 | tf_op jit(solution)/shard_map/reduce_scatter | solution.py:300
  258.3 5.1 %collective-permute-start = (bf16[512,128]{1,0:T(8,128)(2,1)}, bf16[512,128]{1,0:T(8,128)(2,1)S(1)}, u32[]{:S(2)}, u32[]{:S(2)}) collective-permute-start(bf16[512,128]{1,0:T(8,128)(2,1)} %bitcast.10), channel_id=1, source_target_pairs={{0,0},{1,1},{2,2},{3,3},{4,36},{5,37},{6,38},{7,39},{8,72},{9,73},... | collective-permute-start | bytes 393224 | tf_op jit(solution)/shard_map/ppermute | solution.py:303
  263.4 3.0 %all-to-all-done.4.kv1_ref = bf16[32,128,128]{2,1,0:T(8,128)(2,1)S(1)} async-done(((bf16[32,128,128]{2,1,0:T(8,128)(2,1)}), bf16[32,128,128]{2,1,0:T(8,128)(2,1)S(1)}, u32[]{:S(2)}, u32[]{:S(2)}) %all-to-all-start.4) | async-done | bytes 1048608 | tf_op jit(solution)/shard_map/all_to_all | solution.py:274
  266.4 2.1 unpack.1.refs_1_
  268.5 0.8 collective-permute-done
  269.3 0.7 copy-done.3
  269.9 2.5 grams.1
  (11 shorter events, 0.1 us)
Async XLA Ops:
  7.2 192.0 %all-gather.2.cloned.1.call-start = ((), (), s32[]{:S(2)}) async-start(), calls=%async_computation.7 | async-start | bytes 34603008 | tf_op jit(solution)/shard_map/all_gather | solution.py:286
  10.6 60.2 %all-to-all-start.1 = ((bf16[32,256,128]{2,1,0:T(8,128)(2,1)}), bf16[32,256,128]{2,1,0:T(8,128)(2,1)S(1)}, u32[]{:S(2)}, u32[]{:S(2)}) async-start(bf16[32,256,128]{2,1,0:T(8,128)(2,1)} %pack0.1), calls=%async_computation.1 | async-start | bytes 4194304 | tf_op jit(solution)/shard_map/all_to_all | solution.py:274
  70.8 4.6 %copy-start.2 = (bf16[32,256,128]{2,1,0:T(8,128)(2,1)}, bf16[32,256,128]{2,1,0:T(8,128)(2,1)S(1)}, u32[]{:S(2)}) copy-start(bf16[32,256,128]{2,1,0:T(8,128)(2,1)S(1)} %all-to-all-done.1.recv_ref) | copy-start | bytes 6291460
  70.8 55.1 %all-to-all-start = ((bf16[32,256,128]{2,1,0:T(8,128)(2,1)}), bf16[32,256,128]{2,1,0:T(8,128)(2,1)}, u32[]{:S(2)}, u32[]{:S(2)}) async-start(bf16[32,256,128]{2,1,0:T(8,128)(2,1)} %pack1.1), calls=%async_computation | async-start | bytes 4194304 | tf_op jit(solution)/shard_map/all_to_all | solution.py:274
  192.5 34.8 %all-to-all-start.3 = ((bf16[32,128,128]{2,1,0:T(8,128)(2,1)}), bf16[32,128,128]{2,1,0:T(8,128)(2,1)S(1)}, u32[]{:S(2)}, u32[]{:S(2)}) async-start(bf16[32,128,128]{2,1,0:T(8,128)(2,1)} %get-tuple-element.11), calls=%async_computation.3 | async-start | bytes 2097152 | tf_op jit(solution)/shard_map/all_to_all | solution.py:274
  199.1 59.2 %reduce-scatter.2.cloned.1.call-start = ((), (), s32[]{:S(2)}) async-start(), calls=%async_computation.8 | async-start | bytes 1179648 | tf_op jit(solution)/shard_map/reduce_scatter | solution.py:300
  227.3 1.0 copy-start
  228.2 38.2 %copy-start.1 = (bf16[32,128,128]{2,1,0:T(8,128)(2,1)S(1)}, bf16[32,128,128]{2,1,0:T(8,128)(2,1)}, u32[]{:S(2)}) copy-start(bf16[32,128,128]{2,1,0:T(8,128)(2,1)} %copy-done) | copy-start | bytes 3145732
  228.2 38.2 %all-to-all-start.4 = ((bf16[32,128,128]{2,1,0:T(8,128)(2,1)}), bf16[32,128,128]{2,1,0:T(8,128)(2,1)S(1)}, u32[]{:S(2)}, u32[]{:S(2)}) async-start(bf16[32,128,128]{2,1,0:T(8,128)(2,1)} %after.2), calls=%async_computation.4 | async-start | bytes 2097152 | tf_op jit(solution)/shard_map/all_to_all | solution.py:274
  258.3 11.0 %collective-permute-start = (bf16[512,128]{1,0:T(8,128)(2,1)}, bf16[512,128]{1,0:T(8,128)(2,1)S(1)}, u32[]{:S(2)}, u32[]{:S(2)}) collective-permute-start(bf16[512,128]{1,0:T(8,128)(2,1)} %bitcast.10), channel_id=1, source_target_pairs={{0,0},{1,1},{2,2},{3,3},{4,36},{5,37},{6,38},{7,39},{8,72},{9,73},... | collective-permute-start | bytes 393224 | tf_op jit(solution)/shard_map/ppermute | solution.py:303
  269.3 0.7 copy-start.3
Sparse Core Ops, SparseCore 0:
  10.6 169.0 all-gather.1
  212.9 45.3 reduce-scatter.1

commit v6 on v5

--- a/solution.py
+++ b/solution.py
@@ -262,7 +262,7 @@
         in_specs=[vmem] * 3,
         out_specs=[vmem] * 2,
         out_shape=[shape, shape],
-        compiler_params=pltpu.CompilerParams(vmem_limit_bytes=VMEM),
+        compiler_params=pltpu.CompilerParams(vmem_limit_bytes=4 << 20),
         name="grams",
         cost_estimate=pl.CostEstimate(
             flops=6 * 16 * HDIM**3, bytes_accessed=1 << 20, transcendentals=0

time: 281 us -> 281 us (level)
  no operation moved by 1% of the time
where the time goes in v6:
time: 281 us; the launch traced here: 279 us
  waiting for transfers between devices  129 us (46%)
  blocking collectives  53.5 us (19%)
  Pallas kernels  49.1 us (17%)
  starting transfers between devices  30.7 us (11%)
  between operations  14.1 us (5%)
    all_to_all x4, waiting for transfers between devices, swap(): return lax.all_to_all(value, axes, split_axis=0, concat_axis=0, tiled=True)  103 us
    all_to_all x2, blocking collectives, swap(): return lax.all_to_all(value, axes, split_axis=0, concat_axis=0, tiled=True)  53.5 us
    pallas_call x2, Pallas kernels, attention(): pl.pallas_call(functools.partial(attention_kernel, seq), in_specs=[vmem]...  26.5 us
    all_to_all x4, starting transfers between devices, swap(): return lax.all_to_all(value, axes, split_axis=0, concat_axis=0, tiled=True)  25.9 us
    reduce_scatter x1, waiting for transfers between devices, on_device(): lax.psum_scatter(partial.reshape(N_Z, SPAN * HDIM, HDIM), 'z', scatter_di...  25.2 us
    pallas_call x1, Pallas kernels, tile_sums(): pl.pallas_call(tiles_kernel, grid=(N_CTX * HDIM // FEATS,), in_specs=[pl....  13.6 us
  transfers between devices with their start and end apart: 7, of which 6 were waited for; matrix products, arithmetic and copies ran while one was open for 0% of the time, Pallas kernels for 17%

profile of v6, /device:TPU:46, one launch (start us, length us, event | category | flops | bytes accessed | tf_op | source)
XLA Modules:
  0.0 279.3 jit_solution(15601554456568054850)
XLA Ops:
  7.2 0.7 all-gather.2.cloned.1.call-update
  7.9 2.7 pack0.1
  10.6 9.6 %all-to-all-start.1 = ((bf16[32,256,128]{2,1,0:T(8,128)(2,1)}), bf16[32,256,128]{2,1,0:T(8,128)(2,1)S(1)}, u32[]{:S(2)}, u32[]{:S(2)}) async-start(bf16[32,256,128]{2,1,0:T(8,128)(2,1)} %pack0.1), calls=%async_computation.1 | async-start | bytes 4194304 | tf_op jit(solution)/shard_map/all_to_all | solution.py:274
  20.2 2.7 pack1.1
  22.9 47.8 %all-to-all-done.1.recv_ref = bf16[32,256,128]{2,1,0:T(8,128)(2,1)S(1)} async-done(((bf16[32,256,128]{2,1,0:T(8,128)(2,1)}), bf16[32,256,128]{2,1,0:T(8,128)(2,1)S(1)}, u32[]{:S(2)}, u32[]{:S(2)}) %all-to-all-start.1) | async-done | bytes 2097184 | tf_op jit(solution)/shard_map/all_to_all | solution.py:274
  70.8 4.6 %all-to-all-start = ((bf16[32,256,128]{2,1,0:T(8,128)(2,1)}), bf16[32,256,128]{2,1,0:T(8,128)(2,1)}, u32[]{:S(2)}, u32[]{:S(2)}) async-start(bf16[32,256,128]{2,1,0:T(8,128)(2,1)} %pack1.1), calls=%async_computation | async-start | bytes 4194304 | tf_op jit(solution)/shard_map/all_to_all | solution.py:274
  75.3 13.4 %attention0.1 = (bf16[32,64,128]{2,1,0:T(8,128)(2,1)}, bf16[32,128,128]{2,1,0:T(8,128)(2,1)}) custom-call(bf16[32,256,128]{2,1,0:T(8,128)(2,1)} %copy-done.6, f32[3,3,128]{2,1,0:T(4,128)} %taps_ref.3), custom_call_target="tpu_custom_call" | custom-call | flops 3221225472 | bytes 4194304 | tf_op jit(solution)/shard_map/attention0/pallas_call | solution.py:142
  88.7 37.1 %all-to-all-done.recv_ref = bf16[32,256,128]{2,1,0:T(8,128)(2,1)} async-done(((bf16[32,256,128]{2,1,0:T(8,128)(2,1)}), bf16[32,256,128]{2,1,0:T(8,128)(2,1)}, u32[]{:S(2)}, u32[]{:S(2)}) %all-to-all-start) | async-done | bytes 2097184 | tf_op jit(solution)/shard_map/all_to_all | solution.py:274
  125.8 13.2 %attention1.1 = (bf16[32,128,128]{2,1,0:T(8,128)(2,1)}, bf16[32,128,128]{2,1,0:T(8,128)(2,1)}) custom-call(bf16[32,256,128]{2,1,0:T(8,128)(2,1)} %all-to-all-done.recv_ref, f32[3,3,128]{2,1,0:T(4,128)} %taps_ref.3, bf16[32,64,128]{2,1,0:T(8,128)(2,1)} %get-tuple-element.9.rest_0_), custom_call_target="tpu_custom_call" | custom-call | flops 3221225472 | bytes 4194304 | tf_op jit(solution)/shard_map/attention1/pallas_call | solution.py:142
  139.0 32.5 %all_to_all.30.q_ref = bf16[32,128,128]{2,1,0:T(8,128)(2,1)S(1)} all-to-all(bf16[32,128,128]{2,1,0:T(8,128)(2,1)} %get-tuple-element.10), channel_id=1, replica_groups=mesh['x'=4,'yh'=2,'z'=8,'yl'=2,'core'=2] {'z','yl','core'}, dimensions={0} | all-to-all | bytes 2097152 | tf_op jit(solution)/shard_map/all_to_all | solution.py:274
  171.5 21.0 %all_to_all.31.grad_ref = bf16[32,128,128]{2,1,0:T(8,128)(2,1)} all-to-all(bf16[32,128,128]{2,1,0:T(8,128)(2,1)S(1)} %all_to_all.30.q_ref), channel_id=1, replica_groups=mesh['x'=4,'yh'=2,'z'=8,'yl'=2,'core'=2] {'x','yh','yl','core'}, dimensions={0} | all-to-all | bytes 2097152 | tf_op jit(solution)/shard_map/all_to_all | solution.py:274
  192.5 6.6 %all-to-all-start.3 = ((bf16[32,128,128]{2,1,0:T(8,128)(2,1)}), bf16[32,128,128]{2,1,0:T(8,128)(2,1)S(1)}, u32[]{:S(2)}, u32[]{:S(2)}) async-start(bf16[32,128,128]{2,1,0:T(8,128)(2,1)} %get-tuple-element.11), calls=%async_computation.3 | async-start | bytes 2097152 | tf_op jit(solution)/shard_map/all_to_all | solution.py:274
  199.2 13.6 %tiles.1 = bf16[32,128,128]{2,1,0:T(8,128)(2,1)} custom-call(s32[1]{0:T(128)} %bitcast.lane_ref, bf16[32,128,128]{2,1,0:T(8,128)(2,1)} %all_to_all.31.grad_ref, bf16[32,128,4096]{2,1,0:T(8,128)(2,1)} %bitcast.7), custom_call_target="tpu_custom_call" | custom-call | flops 4294967296 | bytes 35651584 | tf_op jit(solution)/shard_map/tiles/pallas_call | solution.py:224
  212.8 14.5 %all-to-all-done.3.refs_1_.kv0_ref = bf16[32,128,128]{2,1,0:T(8,128)(2,1)S(1)} async-done(((bf16[32,128,128]{2,1,0:T(8,128)(2,1)}), bf16[32,128,128]{2,1,0:T(8,128)(2,1)S(1)}, u32[]{:S(2)}, u32[]{:S(2)}) %all-to-all-start.3) | async-done | bytes 1048608 | tf_op jit(solution)/shard_map/all_to_all | solution.py:274
  227.3 1.0 copy-done
  228.2 5.1 %all-to-all-start.4 = ((bf16[32,128,128]{2,1,0:T(8,128)(2,1)}), bf16[32,128,128]{2,1,0:T(8,128)(2,1)S(1)}, u32[]{:S(2)}, u32[]{:S(2)}) async-start(bf16[32,128,128]{2,1,0:T(8,128)(2,1)} %after.2), calls=%async_computation.4 | async-start | bytes 2097152 | tf_op jit(solution)/shard_map/all_to_all | solution.py:274
  233.4 25.2 %reduce-scatter.2.cloned.1.call-done = bf16[1,512,128]{2,1,0:T(8,128)(2,1)} async-done(((bf16[8,512,128]{2,1,0:T(8,128)(2,1)}), bf16[1,512,128]{2,1,0:T(8,128)(2,1)}) %reduce-scatter.2.cloned.1.call-update) | async-done | bytes 131088 | tf_op jit(solution)/shard_map/reduce_scatter | solution.py:300
  258.5 4.8 %collective-permute-start = (bf16[512,128]{1,0:T(8,128)(2,1)}, bf16[512,128]{1,0:T(8,128)(2,1)S(1)}, u32[]{:S(2)}, u32[]{:S(2)}) collective-permute-start(bf16[512,128]{1,0:T(8,128)(2,1)} %bitcast.10), channel_id=1, source_target_pairs={{0,0},{1,1},{2,2},{3,3},{4,36},{5,37},{6,38},{7,39},{8,72},{9,73},... | collective-permute-start | bytes 393224 | tf_op jit(solution)/shard_map/ppermute | solution.py:303
  263.3 3.1 %all-to-all-done.4.kv1_ref = bf16[32,128,128]{2,1,0:T(8,128)(2,1)S(1)} async-done(((bf16[32,128,128]{2,1,0:T(8,128)(2,1)}), bf16[32,128,128]{2,1,0:T(8,128)(2,1)S(1)}, u32[]{:S(2)}, u32[]{:S(2)}) %all-to-all-start.4) | async-done | bytes 1048608 | tf_op jit(solution)/shard_map/all_to_all | solution.py:274
  266.4 2.1 unpack.1.refs_1_
  268.5 1.0 collective-permute-done
  269.5 0.7 copy-done.2
  270.1 0.9 copy-done.3
  271.0 1.4 grams.1
  (17 shorter events, 0.1 us)
Async XLA Ops:
  7.2 192.0 %all-gather.2.cloned.1.call-start = ((), (), s32[]{:S(2)}) async-start(), calls=%async_computation.7 | async-start | bytes 34603008 | tf_op jit(solution)/shard_map/all_gather | solution.py:286
  10.6 60.2 %all-to-all-start.1 = ((bf16[32,256,128]{2,1,0:T(8,128)(2,1)}), bf16[32,256,128]{2,1,0:T(8,128)(2,1)S(1)}, u32[]{:S(2)}, u32[]{:S(2)}) async-start(bf16[32,256,128]{2,1,0:T(8,128)(2,1)} %pack0.1), calls=%async_computation.1 | async-start | bytes 4194304 | tf_op jit(solution)/shard_map/all_to_all | solution.py:274
  70.8 4.6 %copy-start.6 = (bf16[32,256,128]{2,1,0:T(8,128)(2,1)}, bf16[32,256,128]{2,1,0:T(8,128)(2,1)S(1)}, u32[]{:S(2)}) copy-start(bf16[32,256,128]{2,1,0:T(8,128)(2,1)S(1)} %all-to-all-done.1.recv_ref) | copy-start | bytes 6291460
  70.8 55.1 %all-to-all-start = ((bf16[32,256,128]{2,1,0:T(8,128)(2,1)}), bf16[32,256,128]{2,1,0:T(8,128)(2,1)}, u32[]{:S(2)}, u32[]{:S(2)}) async-start(bf16[32,256,128]{2,1,0:T(8,128)(2,1)} %pack1.1), calls=%async_computation | async-start | bytes 4194304 | tf_op jit(solution)/shard_map/all_to_all | solution.py:274
  192.5 34.8 %all-to-all-start.3 = ((bf16[32,128,128]{2,1,0:T(8,128)(2,1)}), bf16[32,128,128]{2,1,0:T(8,128)(2,1)S(1)}, u32[]{:S(2)}, u32[]{:S(2)}) async-start(bf16[32,128,128]{2,1,0:T(8,128)(2,1)} %get-tuple-element.11), calls=%async_computation.3 | async-start | bytes 2097152 | tf_op jit(solution)/shard_map/all_to_all | solution.py:274
  199.1 59.4 %reduce-scatter.2.cloned.1.call-start = ((), (), s32[]{:S(2)}) async-start(), calls=%async_computation.8 | async-start | bytes 1179648 | tf_op jit(solution)/shard_map/reduce_scatter | solution.py:300
  227.3 1.0 copy-start
  228.2 38.1 %copy-start.1 = (bf16[32,128,128]{2,1,0:T(8,128)(2,1)S(1)}, bf16[32,128,128]{2,1,0:T(8,128)(2,1)}, u32[]{:S(2)}) copy-start(bf16[32,128,128]{2,1,0:T(8,128)(2,1)} %copy-done) | copy-start | bytes 3145732
  228.2 38.1 %all-to-all-start.4 = ((bf16[32,128,128]{2,1,0:T(8,128)(2,1)}), bf16[32,128,128]{2,1,0:T(8,128)(2,1)S(1)}, u32[]{:S(2)}, u32[]{:S(2)}) async-start(bf16[32,128,128]{2,1,0:T(8,128)(2,1)} %after.2), calls=%async_computation.4 | async-start | bytes 2097152 | tf_op jit(solution)/shard_map/all_to_all | solution.py:274
  258.5 11.0 %collective-permute-start = (bf16[512,128]{1,0:T(8,128)(2,1)}, bf16[512,128]{1,0:T(8,128)(2,1)S(1)}, u32[]{:S(2)}, u32[]{:S(2)}) collective-permute-start(bf16[512,128]{1,0:T(8,128)(2,1)} %bitcast.10), channel_id=1, source_target_pairs={{0,0},{1,1},{2,2},{3,3},{4,36},{5,37},{6,38},{7,39},{8,72},{9,73},... | collective-permute-start | bytes 393224 | tf_op jit(solution)/shard_map/ppermute | solution.py:303
  268.5 1.7 copy-start.4
  268.5 1.7 copy-start.5
  269.5 0.7 copy-start.2
  270.1 0.9 copy-start.3
Sparse Core Ops, SparseCore 0:
  10.6 169.0 all-gather.1
  212.9 45.5 reduce-scatter.1
